TPU v7x, 128 devices: a whole 4x4x4 slice. The times are simulated.
128 devices in a mesh: ctx: 16 (over y, x), shard: 8 (over z, core).
Axes of the slice: x: 4, y: 4, z: 4, core: 2. Of those that a mesh axis runs over, the one named last changes fastest.
Arguments:
- tokens: bfloat16 [16384, 768], P(('ctx', 'shard')), may hold values from -6 to 6
- span_order: int32 [32], replicated, may hold values from 0 to 31, as said below
- first_gain: bfloat16 [768], P('shard'), may hold values from 0.5 to 1.5
- first_shift: bfloat16 [768], P('shard'), may hold values from -3 to 3
- query_weight: bfloat16 [768, 768], P('shard'), may hold values from -0.4375 to 0.4375
- query_bias: bfloat16 [768], P('shard'), may hold values from -3 to 3
- key_weight: bfloat16 [768, 768], P('shard'), may hold values from -0.21875 to 0.21875
- value_weight: bfloat16 [768, 768], P('shard'), may hold values from -0.21875 to 0.21875
- value_bias: bfloat16 [768], P('shard'), may hold values from -3 to 3
- out_weight: bfloat16 [768, 768], P('shard'), may hold values from -3.5 to 3.5
- out_bias: bfloat16 [768], P('shard'), may hold values from -3 to 3
- second_gain: bfloat16 [768], P('shard'), may hold values from 0.5 to 1.5
- second_shift: bfloat16 [768], P('shard'), may hold values from -3 to 3
- up_weight: bfloat16 [768, 3072], P('shard'), may hold values from -0.21875 to 0.21875
- up_bias: bfloat16 [3072], P('shard'), may hold values from -3 to 3
- down_weight: bfloat16 [3072, 768], P('shard'), may hold values from -0.109375 to 0.109375
- down_bias: bfloat16 [768], P('shard'), may hold values from -3 to 3
- cotangent: bfloat16 [16384, 768], P(('ctx', 'shard')), may hold values from -6 to 6
Outputs:
- activations: bfloat16 [16384, 768], P(('ctx', 'shard'))
- input_grad: float32 [16384, 768], P(('ctx', 'shard'))
- grad_first_gain: float32 [768], P('shard')
- grad_first_shift: float32 [768], P('shard')
- grad_query_weight: float32 [768, 768], P('shard')
- grad_query_bias: float32 [768], P('shard')
- grad_key_weight: float32 [768, 768], P('shard')
- grad_value_weight: float32 [768, 768], P('shard')
- grad_value_bias: float32 [768], P('shard')
- grad_out_weight: float32 [768, 768], P('shard')
- grad_out_bias: float32 [768], P('shard')
- grad_second_gain: float32 [768], P('shard')
- grad_second_shift: float32 [768], P('shard')
- grad_up_weight: float32 [768, 3072], P('shard')
- grad_up_bias: float32 [3072], P('shard')
- grad_down_weight: float32 [3072, 768], P('shard')
- grad_down_bias: float32 [768], P('shard')
Inputs may be any that keep to these rules, and one draw needn't show every extreme that they name: span_order is a permutation of the 32 span numbers in which entries 2c and 2c + 1 add up to 31.
All inputs are finite; a program needn't handle non-finite values.
Results may differ from a plain program's by a relative error of at most 0.04.
Values may be sent and summed in bfloat16 or wider, within the bound.
No kernel may reach another device: no remote copies, remote signals or barrier semaphores. Data moves between devices by JAX's collectives and lax.ppermute only.
A program may use at most 192 MiB of HBM per device.

v0:
```python
import jax
import jax.numpy as jnp
from jax import lax
from jax.sharding import PartitionSpec as P

HEAD_DIM = 64


norm_eps = 1e-05
masked_score = -1e30


def joined(x, axis, combine):
    everything = jax.tree.map(lambda part: lax.all_gather(part, axis), x)
    initial = jax.tree.map(lambda part: part[0], everything)

    def hop(k, so_far):
        return combine(so_far, jax.tree.map(lambda part: part[k], everything))

    return lax.fori_loop(1, lax.axis_size(axis), hop, initial)


def as_sent(x):

    def short(part):
        return part.astype(jnp.bfloat16) if part.dtype == jnp.float32 else part

    return jax.tree.map(short, x)


def norm_rows(values, gain, shift):
    center = values - jnp.mean(values, axis=-1, keepdims=True)
    spread = jnp.mean(center * center, axis=-1, keepdims=True)
    return center * lax.rsqrt(spread + norm_eps) * gain + shift


def dense(left, right):
    return jnp.dot(left, right, preferred_element_type=jnp.float32)


def contract_rows(left, right):
    return lax.dot_general(
        left, right, (((0,), (0,)), ((), ())), preferred_element_type=jnp.float32
    )


def contract_cols(left, right):
    return lax.dot_general(
        left, right, (((1,), (1,)), ((), ())), preferred_element_type=jnp.float32
    )


def lookup_place(stored, span_order, span_rows):
    span_ids = jnp.arange(span_order.shape[0], dtype=jnp.int32)
    matches = (stored // span_rows)[:, None] == span_ids[None, :]
    span_start = jnp.sum(jnp.where(matches, span_order[None, :], 0), axis=1)
    return span_start * span_rows + stored % span_rows


def masked_scores(query_blk, key_blk, query_mark, key_mark):
    scores = jnp.einsum("qhd,khd->hqk", query_blk, key_blk, preferred_element_type=jnp.float32)
    allowed = key_mark[None, None, :] <= query_mark[None, :, None]
    return (jnp.where(allowed, scores, masked_score), allowed)


def combine_stats(former, latter):
    highest_seen = jnp.maximum(former[0], latter[0])
    return (
        highest_seen,
        former[1] * jnp.exp(former[0] - highest_seen)
        + latter[1] * jnp.exp(latter[0] - highest_seen),
    )


def keep_state(state):
    return state


def on_device(
    tokens,
    span_order,
    first_gain,
    first_shift,
    query_weight,
    query_bias,
    key_weight,
    value_weight,
    value_bias,
    out_weight,
    out_bias,
    second_gain,
    second_shift,
    up_weight,
    up_bias,
    down_weight,
    down_bias,
    cotangent,
):
    shard_count = lax.axis_size("shard")
    context_count = lax.axis_size("ctx")
    token_rows = tokens.shape[0]
    model_width = tokens.shape[1]
    head_count = model_width // HEAD_DIM
    gathered = (
        lax.all_gather(first_gain, "shard", axis=0, tiled=True),
        lax.all_gather(first_shift, "shard", axis=0, tiled=True),
        lax.all_gather(query_weight, "shard", axis=0, tiled=True),
        lax.all_gather(query_bias, "shard", axis=0, tiled=True),
        lax.all_gather(key_weight, "shard", axis=0, tiled=True),
        lax.all_gather(value_weight, "shard", axis=0, tiled=True),
        lax.all_gather(value_bias, "shard", axis=0, tiled=True),
        lax.all_gather(out_weight, "shard", axis=0, tiled=True),
        lax.all_gather(out_bias, "shard", axis=0, tiled=True),
        lax.all_gather(second_gain, "shard", axis=0, tiled=True),
        lax.all_gather(second_shift, "shard", axis=0, tiled=True),
        lax.all_gather(up_weight, "shard", axis=0, tiled=True),
        lax.all_gather(up_bias, "shard", axis=0, tiled=True),
        lax.all_gather(down_weight, "shard", axis=0, tiled=True),
        lax.all_gather(down_bias, "shard", axis=0, tiled=True),
    )
    (
        gain_one,
        shift_one,
        w_query,
        b_query,
        w_key,
        w_value,
        b_value,
        w_out,
        b_out,
        gain_two,
        shift_two,
        w_up,
        b_up,
        w_down,
        b_down,
    ) = gathered
    tokens_f = tokens.astype(jnp.float32)
    normed, first_back = jax.vjp(
        norm_rows, tokens_f, gain_one.astype(jnp.float32), shift_one.astype(jnp.float32)
    )
    normed_low = normed.astype(jnp.bfloat16)
    queries = ((dense(normed_low, w_query) + b_query.astype(jnp.float32)) * 0.125).astype(
        jnp.bfloat16
    )
    keyset = dense(normed_low, w_key).astype(jnp.bfloat16)
    valueset = (dense(normed_low, w_value) + b_value.astype(jnp.float32)).astype(jnp.bfloat16)
    span_rows = token_rows * shard_count // 2
    query_count = shard_count * token_rows
    key_count = context_count * token_rows
    query_stored = lax.axis_index("ctx") * query_count + jnp.arange(query_count, dtype=jnp.int32)
    query_place = lookup_place(query_stored, span_order, span_rows)
    key_stored = (
        jnp.arange(context_count, dtype=jnp.int32)[:, None] * shard_count + lax.axis_index("shard")
    ) * token_rows + jnp.arange(token_rows, dtype=jnp.int32)[None, :]
    key_place = lookup_place(key_stored.reshape(-1), span_order, span_rows)
    query_all = lax.all_gather(queries, "shard", axis=0, tiled=True)
    key_all, value_all = (
        lax.all_gather(keyset, "ctx", axis=0, tiled=True),
        lax.all_gather(valueset, "ctx", axis=0, tiled=True),
    )
    query_block = 512
    key_block = 256
    query_blocks = query_count // query_block
    key_blocks = key_count // key_block
    query_split = query_all.reshape(query_blocks, query_block, head_count, HEAD_DIM)
    query_marks = query_place.reshape(query_blocks, query_block)
    key_split = key_all.reshape(key_blocks, key_block, head_count, HEAD_DIM)
    value_split = value_all.reshape(key_blocks, key_block, head_count, HEAD_DIM)
    key_marks = key_place.reshape(key_blocks, key_block)

    def block_stats(block_entry):
        query_blk, query_mark = block_entry
        latest = jnp.max(query_mark)

        def visit(carry, key_entry):
            key_blk, key_mark = key_entry

            def update(state):
                best_seen, total_seen = state
                scores, allowed = masked_scores(query_blk, key_blk, query_mark, key_mark)
                new_best = jnp.maximum(best_seen, jnp.max(scores, axis=2))
                grown = jnp.sum(
                    jnp.where(allowed, jnp.exp(scores - new_best[:, :, None]), 0.0), axis=2
                )
                return (new_best, total_seen * jnp.exp(best_seen - new_best) + grown)

            return (lax.cond(jnp.min(key_mark) <= latest, update, keep_state, carry), None)

        initial = (
            jnp.full((head_count, query_block), masked_score, jnp.float32),
            jnp.zeros((head_count, query_block), jnp.float32),
        )
        finished, unused = lax.scan(visit, initial, (key_split, key_marks))
        return finished

    best_all, total_all = lax.map(block_stats, (query_split, query_marks))
    best_all, total_all = joined((best_all, total_all), "shard", combine_stats)
    log_total = best_all + jnp.log(total_all)

    def block_values(block_entry):
        query_blk, query_mark, log_blk = block_entry
        latest = jnp.max(query_mark)

        def visit(carry, key_entry):
            key_blk, value_blk, key_mark = key_entry

            def update(state):
                coarse, finer = state
                scores, allowed = masked_scores(query_blk, key_blk, query_mark, key_mark)
                weights = jnp.exp(scores - log_blk[:, :, None])
                rough = weights.astype(jnp.bfloat16)
                residue = (weights - rough.astype(jnp.float32)).astype(jnp.bfloat16)
                main_part = jnp.einsum(
                    "hqk,khd->qhd", rough, value_blk, preferred_element_type=jnp.float32
                )
                extra_part = jnp.einsum(
                    "hqk,khd->qhd", residue, value_blk, preferred_element_type=jnp.float32
                )
                return (coarse + main_part, finer + main_part + extra_part)

            return (lax.cond(jnp.min(key_mark) <= latest, update, keep_state, carry), None)

        zero_block = jnp.zeros((query_block, head_count, HEAD_DIM), jnp.float32)
        finished, unused = lax.scan(
            visit, (zero_block, zero_block), (key_split, value_split, key_marks)
        )
        return finished

    coarse_all, finer_all = lax.map(block_values, (query_split, query_marks, log_total))
    coarse_own, finer_own = (
        lax.psum_scatter(
            coarse_all.reshape(query_count, model_width).astype(jnp.bfloat16),
            "shard",
            scatter_dimension=0,
            tiled=True,
        ).astype(jnp.float32),
        lax.psum_scatter(
            finer_all.reshape(query_count, model_width).astype(jnp.bfloat16),
            "shard",
            scatter_dimension=0,
            tiled=True,
        ).astype(jnp.float32),
    )
    context_low = coarse_own.astype(jnp.bfloat16)
    middle = tokens_f + dense(context_low, w_out) + b_out.astype(jnp.float32)
    second, second_back = jax.vjp(
        norm_rows, middle, gain_two.astype(jnp.float32), shift_two.astype(jnp.float32)
    )
    second_low = second.astype(jnp.bfloat16)
    pre_act = dense(second_low, w_up) + b_up.astype(jnp.float32)
    hidden, gelu_back = jax.vjp(jax.nn.gelu, pre_act)
    hidden_low = hidden.astype(jnp.bfloat16)
    activations = (middle + dense(hidden_low, w_down) + b_down.astype(jnp.float32)).astype(
        jnp.bfloat16
    )
    upstream = cotangent.astype(jnp.float32)
    grad_down_bias = jnp.sum(upstream, axis=0)
    dpre = gelu_back(contract_cols(cotangent, w_down))[0].astype(jnp.bfloat16)
    grad_up_bias = jnp.sum(dpre.astype(jnp.float32), axis=0)
    dmid_norm, grad_second_gain, grad_second_shift = second_back(contract_cols(dpre, w_up))
    dmiddle = upstream + dmid_norm
    dmid_low = dmiddle.astype(jnp.bfloat16)
    grad_out_bias = jnp.sum(dmid_low.astype(jnp.float32), axis=0)
    dcontext = contract_cols(dmid_low, w_out).astype(jnp.bfloat16)
    dcontext_f = dcontext.astype(jnp.float32)
    delta_own = jnp.sum(
        (dcontext_f * finer_own).reshape(token_rows, head_count, HEAD_DIM), axis=2
    ).T
    dcontext_all, delta_all = (
        lax.all_gather(dcontext_f.astype(jnp.bfloat16), "shard", axis=0, tiled=True).astype(
            dcontext_f.dtype
        ),
        lax.all_gather(delta_own.astype(jnp.bfloat16), "shard", axis=1, tiled=True).astype(
            delta_own.dtype
        ),
    )
    dcontext_split = dcontext_all.astype(jnp.bfloat16).reshape(
        query_blocks, query_block, head_count, HEAD_DIM
    )
    delta_split = jnp.swapaxes(delta_all.reshape(head_count, query_blocks, query_block), 0, 1)

    def block_grads(carry, block_entry):
        key_acc, value_acc = carry
        query_blk, query_mark, log_blk, dctx_blk, delta_blk = block_entry
        latest = jnp.max(query_mark)

        def visit(dquery_acc, key_entry):
            key_blk, value_blk, key_mark = key_entry

            def update(acc):
                scores, allowed = masked_scores(query_blk, key_blk, query_mark, key_mark)
                weights = jnp.exp(scores - log_blk[:, :, None])
                rough = weights.astype(jnp.bfloat16)
                dvalue_blk = jnp.einsum(
                    "hqk,qhd->khd", rough, dctx_blk, preferred_element_type=jnp.float32
                )
                dweights = jnp.einsum(
                    "qhd,khd->hqk", dctx_blk, value_blk, preferred_element_type=jnp.float32
                )
                dscore = (weights * (dweights - delta_blk[:, :, None])).astype(jnp.bfloat16)
                new_acc = acc + jnp.einsum(
                    "hqk,khd->qhd", dscore, key_blk, preferred_element_type=jnp.float32
                )
                dkey_blk = jnp.einsum(
                    "hqk,qhd->khd", dscore, query_blk, preferred_element_type=jnp.float32
                )
                return (new_acc, dkey_blk, dvalue_blk)

            def skipped(acc):
                empty_keys = jnp.zeros((key_block, head_count, HEAD_DIM), jnp.float32)
                return (acc, empty_keys, empty_keys)

            new_acc, dkey_blk, dvalue_blk = lax.cond(
                jnp.min(key_mark) <= latest, update, skipped, dquery_acc
            )
            return (new_acc, (dkey_blk, dvalue_blk))

        zero_block = jnp.zeros((query_block, head_count, HEAD_DIM), jnp.float32)
        dquery_blk, (dkey_all, dvalue_all) = lax.scan(
            visit, zero_block, (key_split, value_split, key_marks)
        )
        return ((key_acc + dkey_all, value_acc + dvalue_all), dquery_blk)

    zero_keys = jnp.zeros((key_blocks, key_block, head_count, HEAD_DIM), jnp.float32)
    (dkey_part, dvalue_part), dquery_part = lax.scan(
        block_grads,
        (zero_keys, zero_keys),
        (query_split, query_marks, log_total, dcontext_split, delta_split),
    )
    dquery_own = lax.psum_scatter(
        dquery_part.reshape(query_count, model_width).astype(jnp.bfloat16),
        "shard",
        scatter_dimension=0,
        tiled=True,
    )
    dkey_own, dvalue_own = (
        lax.psum_scatter(
            dkey_part.reshape(key_count, model_width).astype(jnp.bfloat16),
            "ctx",
            scatter_dimension=0,
            tiled=True,
        ).astype(jnp.float32),
        lax.psum_scatter(
            dvalue_part.reshape(key_count, model_width).astype(jnp.bfloat16),
            "ctx",
            scatter_dimension=0,
            tiled=True,
        ).astype(jnp.float32),
    )
    dquery_low = dquery_own * jnp.bfloat16(0.125)
    dkey_low = dkey_own.astype(jnp.bfloat16)
    dvalue_low = dvalue_own.astype(jnp.bfloat16)
    grad_query_bias = jnp.sum(dquery_low.astype(jnp.float32), axis=0)
    grad_value_bias = jnp.sum(dvalue_low.astype(jnp.float32), axis=0)
    dnormed = (
        contract_cols(dquery_low, w_query)
        + contract_cols(dkey_low, w_key)
        + contract_cols(dvalue_low, w_value)
    )
    dtok_norm, grad_first_gain, grad_first_shift = first_back(dnormed)
    input_grad = dmiddle + dtok_norm
    partial_sums = None
    totals = None
    partial_sums = jax.tree.map(
        lambda part: part.astype(jnp.float32),
        lax.psum_scatter(
            as_sent(
                (
                    grad_first_gain,
                    grad_first_shift,
                    contract_rows(normed_low, dquery_low),
                    grad_query_bias,
                    contract_rows(normed_low, dkey_low),
                    contract_rows(normed_low, dvalue_low),
                    grad_value_bias,
                    contract_rows(context_low, dmid_low),
                    grad_out_bias,
                    grad_second_gain,
                    grad_second_shift,
                    contract_rows(second_low, dpre),
                    grad_up_bias,
                    contract_rows(hidden_low, cotangent),
                    grad_down_bias,
                )
            ),
            "shard",
            scatter_dimension=0,
            tiled=True,
        ),
    )
    totals = (
        lax.psum(partial_sums[0].astype(jnp.bfloat16), "ctx").astype(jnp.float32),
        lax.psum(partial_sums[1].astype(jnp.bfloat16), "ctx").astype(jnp.float32),
        lax.psum(partial_sums[2].astype(jnp.bfloat16), "ctx").astype(jnp.float32),
        lax.psum(partial_sums[3].astype(jnp.bfloat16), "ctx").astype(jnp.float32),
        lax.psum(partial_sums[4].astype(jnp.bfloat16), "ctx").astype(jnp.float32),
        lax.psum(partial_sums[5].astype(jnp.bfloat16), "ctx").astype(jnp.float32),
        lax.psum(partial_sums[6].astype(jnp.bfloat16), "ctx").astype(jnp.float32),
        lax.psum(partial_sums[7].astype(jnp.bfloat16), "ctx").astype(jnp.float32),
        lax.psum(partial_sums[8].astype(jnp.bfloat16), "ctx").astype(jnp.float32),
        lax.psum(partial_sums[9].astype(jnp.bfloat16), "ctx").astype(jnp.float32),
        lax.psum(partial_sums[10].astype(jnp.bfloat16), "ctx").astype(jnp.float32),
        lax.psum(partial_sums[11].astype(jnp.bfloat16), "ctx").astype(jnp.float32),
        lax.psum(partial_sums[12].astype(jnp.bfloat16), "ctx").astype(jnp.float32),
        lax.psum(partial_sums[13].astype(jnp.bfloat16), "ctx").astype(jnp.float32),
        lax.psum(partial_sums[14].astype(jnp.bfloat16), "ctx").astype(jnp.float32),
    )
    return (
        activations,
        input_grad,
        totals[0],
        totals[1],
        totals[2],
        totals[3],
        totals[4],
        totals[5],
        totals[6],
        totals[7],
        totals[8],
        totals[9],
        totals[10],
        totals[11],
        totals[12],
        totals[13],
        totals[14],
    )


def solution(mesh):
    return jax.shard_map(
        on_device,
        mesh=mesh,
        in_specs=(
            P(("ctx", "shard"), None),
            P(),
            P("shard"),
            P("shard"),
            P("shard", None),
            P("shard"),
            P("shard", None),
            P("shard", None),
            P("shard"),
            P("shard", None),
            P("shard"),
            P("shard"),
            P("shard"),
            P("shard", None),
            P("shard"),
            P("shard", None),
            P("shard"),
            P(("ctx", "shard"), None),
        ),
        out_specs=(
            P(("ctx", "shard"), None),
            P(("ctx", "shard"), None),
            P("shard"),
            P("shard"),
            P("shard", None),
            P("shard"),
            P("shard", None),
            P("shard", None),
            P("shard"),
            P("shard", None),
            P("shard"),
            P("shard"),
            P("shard"),
            P("shard", None),
            P("shard"),
            P("shard", None),
            P("shard"),
        ),
        check_vma=False,
    )
```

profile of v0, /device:TPU:0, one launch (start us, length us, event | category | flops | bytes accessed | tf_op | source)
XLA Modules:
  0.0 1339.3 jit_solution(11084315001905453590)
XLA Ops:
  17.3 28.4 %all-reduce.20 = (bf16[768]{0:T(1024)(128)(2,1)S(1)}, bf16[768]{0:T(1024)(128)(2,1)S(1)}, bf16[768]{0:T(1024)(128)(2,1)S(1)}, bf16[768]{0:T(1024)(128)(2,1)S(1)}...) all-reduce(bf16[768]{0:T(1024)(128)(2,1)S(1)} %dynamic-update-slice, ...), channel_id=1, replica_groups=mesh['ctx'=16,'shard'=8] {'shard'}, use_global_device_ids=true, to_apply=%add.2 | all-reduce | flops 5376 | bytes 21504
  50.5 11.1 all-gather.18.cloned.1.call-done
  64.0 23.3 %all-gather.22.cloned.1.call-done = bf16[768,768]{1,0:T(8,128)(2,1)} async-done(((bf16[96,768]{1,0:T(8,128)(2,1)}), bf16[768,768]{1,0:T(8,128)(2,1)}) %all-gather.22.cloned.1.call-update) | async-done | bytes 1179664 | tf_op jit(solution)/shard_map/all_gather | solution.py:110
  91.7 22.2 %all-gather.16.cloned.1.call-done = bf16[1024,768]{1,0:T(8,128)(2,1)} async-done(((bf16[128,768]{1,0:T(8,128)(2,1)}), bf16[1024,768]{1,0:T(8,128)(2,1)}) %all-gather.16.cloned.1.call-update) | async-done | bytes 1572880 | tf_op jit(solution)/shard_map/all_gather | solution.py:157
  118.3 46.0 %all-gather.20.cloned.1.call-done = bf16[2048,768]{1,0:T(8,128)(2,1)} async-done(((bf16[128,768]{1,0:T(8,128)(2,1)}), bf16[2048,768]{1,0:T(8,128)(2,1)}) %all-gather.20.cloned.1.call-update) | async-done | bytes 3145744 | tf_op jit(solution)/shard_map/all_gather | solution.py:159
  170.9 67.9 %while.99 = (s32[]{:T(128)}, f32[2,12,512]{2,1,0:T(8,128)S(1)}, f32[2,12,512]{2,1,0:T(8,128)S(1)}, s32[2,512]{1,0:T(2,128)S(1)}, bf16[2,512,12,64]{1,3,2,0:T(8,1...) while((s32[]{:T(128)}, f32[2,12,512]{2,1,0:T(8,128)S(1)}, ...), condition=%wide.region_13.14_spmd, body=%wide.region_4.13_spmd.sunk | while | flops 210907904 | bytes 16238512 | solution.py:197
  172.8 44.6 %while.105 = (s32[]{:T(128)}, f32[12,512]{1,0:T(8,128)S(1)}, f32[12,512]{1,0:T(8,128)S(1)}, s32[8,256]{1,0:T(8,128)S(1)}, s32[]{:T(128)}, /*index=5*/s32[512]{0:...) while((s32[]{:T(128)}, f32[12,512]{1,0:T(8,128)S(1)}, ...), condition=%wide.region_12.12_spmd, body=%wide.region_6.11_spmd.sunk | while | flops 210907392 | bytes 14481107 | solution.py:194
  219.3 19.4 %while.105 = (s32[]{:T(128)}, f32[12,512]{1,0:T(8,128)S(1)}, f32[12,512]{1,0:T(8,128)S(1)}, s32[8,256]{1,0:T(8,128)S(1)}, s32[]{:T(128)}, /*index=5*/s32[512]{0:...) while((s32[]{:T(128)}, f32[12,512]{1,0:T(8,128)S(1)}, ...), condition=%wide.region_12.12_spmd, body=%wide.region_6.11_spmd.sunk | while | flops 210907392 | bytes 14481107 | solution.py:194
  238.8 17.1 %all-gather = f32[16,12,512]{2,1,0:T(8,128)S(1)} all-gather(f32[2,12,512]{2,1,0:T(8,128)S(1)} %get-tuple-element.679), channel_id=2, replica_groups=mesh['ctx'=16,'shard'=8] {'shard'}, dimensions={0}, use_global_device_ids=true | all-gather | bytes 442368 | tf_op jit(solution)/shard_map/all_gather | solution.py:14
  256.0 13.7 %all-gather.1 = f32[16,12,512]{2,1,0:T(8,128)S(1)} all-gather(f32[2,12,512]{2,1,0:T(8,128)S(1)} %get-tuple-element.680), channel_id=3, replica_groups=mesh['ctx'=16,'shard'=8] {'shard'}, dimensions={0}, use_global_device_ids=true | all-gather | bytes 442368 | tf_op jit(solution)/shard_map/all_gather | solution.py:14
  279.7 111.7 %while.102 = (s32[]{:T(128)}, bf16[2,512,12,64]{1,3,2,0:T(8,128)(2,1)}, bf16[2,512,12,64]{1,3,2,0:T(8,128)(2,1)}, s32[2,512]{1,0:T(2,128)S(1)}, bf16[2,512,12,64...) while((s32[]{:T(128)}, ...), condition=%wide.region_23.24_spmd, body=%wide.region_16.23_spmd.sunk | while | flops 619447040 | bytes 41790952 | solution.py:230
  282.8 79.0 %while.106 = (s32[]{:T(128)}, f32[512,12,64]{0,2,1:T(8,128)S(1)}, f32[512,12,64]{0,2,1:T(8,128)S(1)}, s32[8,256]{1,0:T(8,128)S(1)}, s32[]{:T(128)}, /*index=5*/s...) while((s32[]{:T(128)}, f32[512,12,64]{0,2,1:T(8,128)S(1)}, ...), condition=%wide.region_22.22_spmd, body=%wide.region_18.21_spmd.sunk | while | flops 619446528 | bytes 30726900 | solution.py:225
  314.3 7.9 conditional.7
  344.0 7.9 conditional.7
  353.9 7.9 conditional.7
  366.3 23.7 %while.106 = (s32[]{:T(128)}, f32[512,12,64]{0,2,1:T(8,128)S(1)}, f32[512,12,64]{0,2,1:T(8,128)S(1)}, s32[8,256]{1,0:T(8,128)S(1)}, s32[]{:T(128)}, /*index=5*/s...) while((s32[]{:T(128)}, f32[512,12,64]{0,2,1:T(8,128)S(1)}, ...), condition=%wide.region_22.22_spmd, body=%wide.region_18.21_spmd.sunk | while | flops 619446528 | bytes 30726900 | solution.py:225
  397.3 19.5 %all-gather.2 = bf16[8,1,384]{2,1,0:T(2,128)(2,1)S(1)} all-gather(bf16[1,1,384]{2,1,0:T(2,128)(2,1)S(1)} %reshape.357), channel_id=1, replica_groups=mesh['ctx'=16,'shard'=8] {'shard'}, dimensions={0}, use_global_device_ids=true | all-gather | bytes 6912 | tf_op jit(solution)/shard_map/all_gather | solution.py:117
  426.6 55.5 %reduce-scatter.34.cloned.1.call-done = bf16[128,768]{1,0:T(8,128)(2,1)} async-done(((bf16[1024,768]{1,0:T(8,128)(2,1)}), bf16[128,768]{1,0:T(8,128)(2,1)}) %reduce-scatter.34.cloned.1.call-update) | async-done | bytes 196624
  484.2 32.7 %all-gather.28.cloned.1.call-done = bf16[768,3072]{1,0:T(8,128)(2,1)} async-done(((bf16[96,3072]{1,0:T(8,128)(2,1)}), bf16[768,3072]{1,0:T(8,128)(2,1)}) %all-gather.28.cloned.1.call-update) | async-done | bytes 4718608 | tf_op jit(solution)/shard_map/all_gather | solution.py:116
  528.6 23.5 %reduce-scatter.20.cloned.1.call-done = bf16[128,768]{1,0:T(8,128)(2,1)} async-done(((bf16[1024,768]{1,0:T(8,128)(2,1)}), bf16[128,768]{1,0:T(8,128)(2,1)}) %reduce-scatter.20.cloned.1.call-update) | async-done | bytes 196624 | tf_op jit(solution)/shard_map/reduce_scatter | solution.py:238
  554.6 11.2 all_gather.95
  565.8 11.8 all-gather.32.cloned.1.call-done
  585.0 189.6 %while.104 = (s32[]{:T(128)}, f32[8,256,12,64]{1,3,2,0:T(8,128)}, f32[8,256,12,64]{1,3,2,0:T(8,128)}, bf16[2,512,12,64]{1,3,2,0:T(8,128)(2,1)}, s32[2,512]{1,0:T...) while((s32[]{:T(128)}, f32[8,256,12,64]{1,3,2,0:T(8,128)}, ...), condition=%wide.region_38.39_spmd.clone, body=%wide.region_31.38_spmd.clone.sunk | while | flops 1026032384 | bytes 143363856 | solution.py:326
  595.2 104.0 %while.107 = (s32[]{:T(128)}, f32[512,12,64]{0,2,1:T(8,128)}, f32[8,256,12,64]{1,3,2,0:T(8,128)}, f32[8,256,12,64]{1,3,2,0:T(8,128)}, s32[8,256]{1,0:T(8,128)S(1...) while((s32[]{:T(128)}, f32[512,12,64]{0,2,1:T(8,128)}, ...), condition=%wide.region_37.37_spmd, body=%wide.region_33.36_spmd.sunk | while | flops 1019740416 | bytes 53558584 | solution.py:320
  597.2 9.8 conditional.6
  610.2 9.8 conditional.6
  623.1 9.8 conditional.6
  636.1 9.8 conditional.6
  649.1 9.8 conditional.6
  662.1 9.8 conditional.6
  675.1 9.8 conditional.6
  688.2 9.8 conditional.6
  699.3 9.7 select_add_fusion.3
  721.3 36.8 %while.107 = (s32[]{:T(128)}, f32[512,12,64]{0,2,1:T(8,128)}, f32[8,256,12,64]{1,3,2,0:T(8,128)}, f32[8,256,12,64]{1,3,2,0:T(8,128)}, s32[8,256]{1,0:T(8,128)S(1...) while((s32[]{:T(128)}, f32[512,12,64]{0,2,1:T(8,128)}, ...), condition=%wide.region_37.37_spmd, body=%wide.region_33.36_spmd.sunk | while | flops 1019740416 | bytes 53558584 | solution.py:320
  726.6 9.8 conditional.6
  758.1 14.4 %select_add_fusion.3 = (f32[8,256,12,64]{1,3,2,0:T(8,128)}, f32[8,256,12,64]{1,3,2,0:T(8,128)}) fusion(f32[8,256,12,64]{1,3,2,0:T(8,128)} %get-tuple-element.1529, f32[8,256,12,64]{1,3,2,0:T(8,128)} %get-tuple-element.1812, pred[]{:T(512)S(6)} %compare.19, f32[8,256,12,64]{1,3,2,0:T(8,128)} %get-tuple-element.1528, ...), kind=kLoop, calls=%fused_computation.80.clone.1 | loop fusion | flops 6291456 | bytes 37748736 | tf_op jit(solution)/shard_map/while/body/eval_jaxpr/add | solution.py:323
  801.2 59.4 %reduce-scatter.36.cloned.1.call-done = bf16[128,768]{1,0:T(8,128)(2,1)} async-done(((bf16[1024,768]{1,0:T(8,128)(2,1)}), bf16[128,768]{1,0:T(8,128)(2,1)}) %reduce-scatter.36.cloned.1.call-update) | async-done | bytes 196624
  872.5 65.8 %reduce-scatter.38.cloned.1.call-done = bf16[128,768]{1,0:T(8,128)(2,1)} async-done(((bf16[2048,768]{1,0:T(8,128)(2,1)}), bf16[128,768]{1,0:T(8,128)(2,1)}) %reduce-scatter.38.cloned.1.call-update) | async-done | bytes 196624
  940.8 75.6 %reduce-scatter.40.cloned.1.call-done = bf16[128,768]{1,0:T(8,128)(2,1)} async-done(((bf16[2048,768]{1,0:T(8,128)(2,1)}), bf16[128,768]{1,0:T(8,128)(2,1)}) %reduce-scatter.40.cloned.1.call-update) | async-done | bytes 196624
  1022.6 27.7 %reduce-scatter.28.cloned.1.call-done = bf16[96,768]{1,0:T(8,128)(2,1)} async-done(((bf16[768,768]{1,0:T(8,128)(2,1)}), bf16[96,768]{1,0:T(8,128)(2,1)}) %reduce-scatter.28.cloned.1.call-update) | async-done | bytes 147472 | tf_op jit(solution)/shard_map/reduce_scatter | solution.py:367
  1050.3 33.9 %reduce-scatter.22.cloned.1.call-done = bf16[96,768]{1,0:T(8,128)(2,1)} async-done(((bf16[768,768]{1,0:T(8,128)(2,1)}), bf16[96,768]{1,0:T(8,128)(2,1)}) %reduce-scatter.22.cloned.1.call-update) | async-done | bytes 147472 | tf_op jit(solution)/shard_map/reduce_scatter | solution.py:367
  1084.2 40.1 %reduce-scatter.30.cloned.1.call-done = bf16[96,3072]{1,0:T(8,128)(2,1)} async-done(((bf16[768,3072]{1,0:T(8,128)(2,1)}), bf16[96,3072]{1,0:T(8,128)(2,1)}) %reduce-scatter.30.cloned.1.call-update) | async-done | bytes 589840 | tf_op jit(solution)/shard_map/reduce_scatter | solution.py:367
  1124.3 40.6 %reduce-scatter.32.cloned.1.call-done = bf16[384,768]{1,0:T(8,128)(2,1)} async-done(((bf16[3072,768]{1,0:T(8,128)(2,1)}), bf16[384,768]{1,0:T(8,128)(2,1)}) %reduce-scatter.32.cloned.1.call-update) | async-done | bytes 589840 | tf_op jit(solution)/shard_map/reduce_scatter | solution.py:367
  1164.9 34.2 %reduce-scatter.24.cloned.1.call-done = bf16[96,768]{1,0:T(8,128)(2,1)} async-done(((bf16[768,768]{1,0:T(8,128)(2,1)}), bf16[96,768]{1,0:T(8,128)(2,1)}) %reduce-scatter.24.cloned.1.call-update) | async-done | bytes 147472 | tf_op jit(solution)/shard_map/reduce_scatter | solution.py:367
  1199.0 33.4 %reduce-scatter.26.cloned.1.call-done = bf16[96,768]{1,0:T(8,128)(2,1)} async-done(((bf16[768,768]{1,0:T(8,128)(2,1)}), bf16[96,768]{1,0:T(8,128)(2,1)}) %reduce-scatter.26.cloned.1.call-update) | async-done | bytes 147472 | tf_op jit(solution)/shard_map/reduce_scatter | solution.py:367
  1237.6 24.1 %all-reduce.19 = (bf16[768]{0:T(1024)(128)(2,1)S(1)}, bf16[768]{0:T(1024)(128)(2,1)S(1)}, bf16[768]{0:T(1024)(128)(2,1)S(1)}, bf16[768]{0:T(1024)(128)(2,1)S(1)}...) all-reduce(bf16[768]{0:T(1024)(128)(2,1)S(1)} %dynamic-update-slice, ...), channel_id=1, replica_groups=mesh['ctx'=16,'shard'=8] {'shard'}, use_global_device_ids=true, to_apply=%add.7 | all-reduce | flops 9984 | bytes 39936
  1262.3 40.9 %all-reduce.17 = (bf16[96]{0:T(256)(128)(2,1)S(1)}, bf16[96]{0:T(256)(128)(2,1)S(1)}, bf16[96]{0:T(256)(128)(2,1)S(1)}, bf16[96]{0:T(256)(128)(2,1)S(1)}, bf16[9...) all-reduce(bf16[96]{0:T(256)(128)(2,1)S(1)} %dynamic-slice.9, ...), channel_id=1, replica_groups=mesh['ctx'=16,'shard'=8] {'ctx'}, use_global_device_ids=true, to_apply=%region_46.47 | all-reduce | flops 1152 | bytes 4608 | tf_op jit(solution)/shard_map/psum | solution.py:393
  1313.2 12.6 all-reduce.23.cloned.1.call-done
  (666 shorter events, 509.9 us)
Async XLA Ops:
  7.2 54.4 %copy-start.5 = (bf16[128,768]{1,0:T(8,128)(2,1)S(1)}, bf16[128,768]{1,0:T(8,128)(2,1)}, u32[]{:S(2)}) copy-start(bf16[128,768]{1,0:T(8,128)(2,1)} %param.38) | copy-start | bytes 589828
  7.2 40.8 %all-gather.14.cloned.1.call-start = ((), (), s32[]{:S(2)}) async-start(), calls=%async_computation.11 | async-start | bytes 1327104 | tf_op jit(solution)/shard_map/all_gather | solution.py:107
  7.9 53.6 %all-gather.18.cloned.1.call-start = ((), (), s32[]{:S(2)}) async-start(), calls=%async_computation.13 | async-start | bytes 1327104 | tf_op jit(solution)/shard_map/all_gather | solution.py:109
  8.7 78.6 %all-gather.22.cloned.1.call-start = ((), (), s32[]{:S(2)}) async-start(), calls=%async_computation.15 | async-start | bytes 1327104 | tf_op jit(solution)/shard_map/all_gather | solution.py:110
  9.4 104.4 %all-gather.16.cloned.1.call-start = ((), (), s32[]{:S(2)}) async-start(), calls=%async_computation.12 | async-start | bytes 1769472 | tf_op jit(solution)/shard_map/all_gather | solution.py:157
  45.7 41.6 %copy-start.28 = (f32[768]{0:T(1024)}, f32[768]{0:T(1024)S(1)}, u32[]{:S(2)}) copy-start(f32[768]{0:T(1024)S(1)} %convert_element_type.264) | copy-start | bytes 9220
  45.7 41.6 %copy-start.38 = (f32[768]{0:T(1024)}, f32[768]{0:T(1024)S(1)}, u32[]{:S(2)}) copy-start(f32[768]{0:T(1024)S(1)} %convert_element_type.265) | copy-start | bytes 9220
  46.8 40.5 %copy-start.40 = (f32[128]{0:T(128)}, f32[128]{0:T(128)S(1)}, u32[]{:S(2)}) copy-start(f32[128]{0:T(128)S(1)} %broadcast_multiply_fusion.3) | copy-start | bytes 1540
  47.9 39.3 %copy-start.42 = (f32[128]{0:T(128)}, f32[128]{0:T(128)S(1)}, u32[]{:S(2)}) copy-start(f32[128]{0:T(128)S(1)} %fusion.95) | copy-start | bytes 1540
  50.5 113.9 %all-gather.20.cloned.1.call-start = ((), (), s32[]{:S(2)}) async-start(), calls=%async_computation.14 | async-start | bytes 3342336 | tf_op jit(solution)/shard_map/all_gather | solution.py:159
  63.9 206.4 %all-gather.24.cloned.1.call-start = ((), (), s32[]{:S(2)}) async-start(), calls=%async_computation.16 | async-start | bytes 3342336 | tf_op jit(solution)/shard_map/all_gather | solution.py:160
  89.6 330.9 %all-gather.30.cloned.1.call-start = ((), (), s32[]{:S(2)}) async-start(), calls=%async_computation.19 | async-start | bytes 5308416 | tf_op jit(solution)/shard_map/all_gather | solution.py:118
  90.4 336.2 %all-gather.26.cloned.1.call-start = ((), (), s32[]{:S(2)}) async-start(), calls=%async_computation.17 | async-start | bytes 1327104 | tf_op jit(solution)/shard_map/all_gather | solution.py:112
  91.1 391.0 %reduce-scatter.34.cloned.1.call-start = ((), (), s32[]{:S(2)}) async-start(), calls=%async_computation.28 | async-start | bytes 1769472
  396.5 120.3 %all-gather.28.cloned.1.call-start = ((), (), s32[]{:S(2)}) async-start(), calls=%async_computation.18 | async-start | bytes 5308416 | tf_op jit(solution)/shard_map/all_gather | solution.py:116
  397.1 155.0 %reduce-scatter.20.cloned.1.call-start = ((), (), s32[]{:S(2)}) async-start(), calls=%async_computation.21 | async-start | bytes 1769472 | tf_op jit(solution)/shard_map/reduce_scatter | solution.py:238
  397.2 129.6 %copy-start.30 = (f32[768]{0:T(1024)}, f32[768]{0:T(1024)S(1)}, u32[]{:S(2)}) copy-start(f32[768]{0:T(1024)S(1)} %convert_element_type.275) | copy-start | bytes 9220
  397.3 119.6 %copy-start.36 = (f32[768]{0:T(1024)}, f32[768]{0:T(1024)S(1)}, u32[]{:S(2)}) copy-start(f32[768]{0:T(1024)S(1)} %convert_element_type.276) | copy-start | bytes 9220
  420.5 61.6 %copy-start.6 = (bf16[128,768]{1,0:T(8,128)(2,1)S(1)}, bf16[128,768]{1,0:T(8,128)(2,1)}, u32[]{:S(2)}) copy-start(bf16[128,768]{1,0:T(8,128)(2,1)} %param.38) | copy-start | bytes 589828
  420.5 157.2 %all-gather.32.cloned.1.call-start = ((), (), s32[]{:S(2)}) async-start(), calls=%async_computation.20 | async-start | bytes 1769472 | tf_op jit(solution)/shard_map/all_gather | solution.py:271
  483.9 42.9 %copy-start.8 = (f32[128,768]{1,0:T(8,128)}, f32[128,768]{1,0:T(8,128)S(1)}, u32[]{:S(2)}) copy-start(f32[128,768]{1,0:T(8,128)S(1)} %get-tuple-element.1045) | copy-start | bytes 1179652
  483.9 42.9 %copy-start.44 = (f32[128]{0:T(128)}, f32[128]{0:T(128)S(1)}, u32[]{:S(2)}) copy-start(f32[128]{0:T(128)S(1)} %broadcast_multiply_fusion.2) | copy-start | bytes 1540
  484.1 42.7 %copy-start.46 = (f32[128]{0:T(128)}, f32[128]{0:T(128)S(1)}, u32[]{:S(2)}) copy-start(f32[128]{0:T(128)S(1)} %fusion.96) | copy-start | bytes 1540
  554.3 306.4 %reduce-scatter.36.cloned.1.call-start = ((), (), s32[]{:S(2)}) async-start(), calls=%async_computation.29 | async-start | bytes 1769472
  779.6 158.6 %reduce-scatter.38.cloned.1.call-start = ((), (), s32[]{:S(2)}) async-start(), calls=%async_computation.30 | async-start | bytes 3342336
  789.2 227.2 %reduce-scatter.40.cloned.1.call-start = ((), (), s32[]{:S(2)}) async-start(), calls=%async_computation.31 | async-start | bytes 3342336
  798.5 63.2 %copy-start.7 = (bf16[128,768]{1,0:T(8,128)(2,1)S(1)}, bf16[128,768]{1,0:T(8,128)(2,1)}, u32[]{:S(2)}) copy-start(bf16[128,768]{1,0:T(8,128)(2,1)} %param.38) | copy-start | bytes 589828
  798.6 63.2 %copy-start.29 = (f32[768]{0:T(1024)S(1)}, f32[768]{0:T(1024)}, u32[]{:S(2)}) copy-start(f32[768]{0:T(1024)} %copy-done.28) | copy-start | bytes 9220
  798.6 63.2 %copy-start.39 = (f32[768]{0:T(1024)S(1)}, f32[768]{0:T(1024)}, u32[]{:S(2)}) copy-start(f32[768]{0:T(1024)} %copy-done.38) | copy-start | bytes 9220
  798.6 63.2 %copy-start.41 = (f32[128]{0:T(128)S(1)}, f32[128]{0:T(128)}, u32[]{:S(2)}) copy-start(f32[128]{0:T(128)} %copy-done.40) | copy-start | bytes 1540
  798.6 63.2 %copy-start.43 = (f32[128]{0:T(128)S(1)}, f32[128]{0:T(128)}, u32[]{:S(2)}) copy-start(f32[128]{0:T(128)} %copy-done.42) | copy-start | bytes 1540
  798.6 251.7 %reduce-scatter.28.cloned.1.call-start = ((), (), s32[]{:S(2)}) async-start(), calls=%async_computation.25 | async-start | bytes 1327104 | tf_op jit(solution)/shard_map/reduce_scatter | solution.py:367
  801.1 62.4 %copy-start.9 = (f32[128,768]{1,0:T(8,128)S(1)}, f32[128,768]{1,0:T(8,128)}, u32[]{:S(2)}) copy-start(f32[128,768]{1,0:T(8,128)} %copy-done.8) | copy-start | bytes 1179652
  801.1 62.4 %copy-start.21 = (bf16[128,3072]{1,0:T(8,128)(2,1)S(1)}, bf16[128,3072]{1,0:T(8,128)(2,1)}, u32[]{:S(2)}) copy-start(bf16[128,3072]{1,0:T(8,128)(2,1)} %copy-done.20) | copy-start | bytes 2359300
  801.1 62.4 %copy-start.31 = (f32[768]{0:T(1024)S(1)}, f32[768]{0:T(1024)}, u32[]{:S(2)}) copy-start(f32[768]{0:T(1024)} %copy-done.30) | copy-start | bytes 9220
  801.1 62.4 %copy-start.37 = (f32[768]{0:T(1024)S(1)}, f32[768]{0:T(1024)}, u32[]{:S(2)}) copy-start(f32[768]{0:T(1024)} %copy-done.36) | copy-start | bytes 9220
  801.1 62.4 %copy-start.45 = (f32[128]{0:T(128)S(1)}, f32[128]{0:T(128)}, u32[]{:S(2)}) copy-start(f32[128]{0:T(128)} %copy-done.44) | copy-start | bytes 1540
  801.2 62.4 %copy-start.47 = (f32[128]{0:T(128)S(1)}, f32[128]{0:T(128)}, u32[]{:S(2)}) copy-start(f32[128]{0:T(128)} %copy-done.46) | copy-start | bytes 1540
  801.2 283.0 %reduce-scatter.22.cloned.1.call-start = ((), (), s32[]{:S(2)}) async-start(), calls=%async_computation.22 | async-start | bytes 1327104 | tf_op jit(solution)/shard_map/reduce_scatter | solution.py:367
  863.4 260.8 %reduce-scatter.30.cloned.1.call-start = ((), (), s32[]{:S(2)}) async-start(), calls=%async_computation.26 | async-start | bytes 5308416 | tf_op jit(solution)/shard_map/reduce_scatter | solution.py:367
  867.2 297.7 %reduce-scatter.32.cloned.1.call-start = ((), (), s32[]{:S(2)}) async-start(), calls=%async_computation.27 | async-start | bytes 5308416 | tf_op jit(solution)/shard_map/reduce_scatter | solution.py:367
  872.4 326.6 %reduce-scatter.24.cloned.1.call-start = ((), (), s32[]{:S(2)}) async-start(), calls=%async_computation.23 | async-start | bytes 1327104 | tf_op jit(solution)/shard_map/reduce_scatter | solution.py:367
  940.8 79.5 %copy-start.62 = (bf16[96]{0:T(256)(128)(2,1)S(1)}, bf16[96]{0:T(256)(128)(2,1)}, u32[]{:S(2)}) copy-start(bf16[96]{0:T(256)(128)(2,1)} %param.54) | copy-start | bytes 580
  940.8 291.6 %reduce-scatter.26.cloned.1.call-start = ((), (), s32[]{:S(2)}) async-start(), calls=%async_computation.24 | async-start | bytes 1327104 | tf_op jit(solution)/shard_map/reduce_scatter | solution.py:367
  1019.0 306.8 %all-reduce.23.cloned.1.call-start = ((), (), s32[]{:S(2)}) async-start(), calls=%async_computation.32 | async-start | bytes 3538944 | tf_op jit(solution)/shard_map/psum | solution.py:395
  1020.8 211.7 %copy-start.26 = (bf16[128,768]{1,0:T(8,128)(2,1)S(1)}, bf16[128,768]{1,0:T(8,128)(2,1)}, u32[]{:S(2)}) copy-start(bf16[128,768]{1,0:T(8,128)(2,1)} %reduce-scatter.38.cloned.1.call-done) | copy-start | bytes 589828
  1235.2 72.8 %copy-start.17 = (f32[128,768]{1,0:T(8,128)S(1)}, f32[128,768]{1,0:T(8,128)}, u32[]{:S(2)}) copy-start(f32[128,768]{1,0:T(8,128)} %copy-done.16) | copy-start | bytes 1179652
  1235.2 72.8 %copy-start.58 = (f32[128]{0:T(128)S(1)}, f32[128]{0:T(128)}, u32[]{:S(2)}) copy-start(f32[128]{0:T(128)} %copy-done.57) | copy-start | bytes 1540
  (58 other events, 288.6 us)
Sparse Core Ops, SparseCore 0:
  9.7 26.2 all-gather.13
  37.7 23.7 all-gather.17
  63.2 23.9 all-gather.21
  89.4 24.4 all-gather.15
  116.4 47.8 all-gather.19
  166.9 46.7 all-gather.23
  215.4 33.4 all-gather.29
  250.6 24.1 all-gather.25
  396.7 85.3 reduce-scatter.33
  483.6 33.2 all-gather.27
  519.3 32.7 reduce-scatter.19
  554.4 23.2 all-gather.31
  779.7 80.9 reduce-scatter.35
  863.8 74.3 reduce-scatter.37
  941.4 74.9 reduce-scatter.39
  1018.6 31.6 reduce-scatter.27
  1053.1 30.9 reduce-scatter.21
  1086.4 37.7 reduce-scatter.29
  1126.7 38.1 reduce-scatter.31
  1167.7 31.3 reduce-scatter.23
  1201.4 30.9 reduce-scatter.25
  1236.5 89.2 all-reduce.22
where the time goes:
time: 1340 us
  waiting for transfers between devices  654 us (49%)
  matrix products  226 us (17%)
  blocking collectives  155 us (12%)
  local copies, waits for them, and re-layouts  123 us (9%)
  other arithmetic  98.2 us (7%)
  loops' own time  65.2 us (5%)
  between operations  17.8 us (1%)
    unnamed x26, waiting for transfers between devices  261 us
    reduce_scatter x6, waiting for transfers between devices, on_device(): lax.psum_scatter(as_sent((grad_first_gain, grad_first_shift, contract_row...  210 us
    dot_general x27, matrix products, masked_scores(): jnp.einsum('qhd,khd->hqk', query_blk, key_blk, preferred_element_type=jnp...  57.5 us
    unnamed x2, blocking collectives  52.4 us
    all_gather x1, waiting for transfers between devices, on_device(): lax.all_gather(keyset, 'ctx', axis=0, tiled=True)  46 us
    psum x1, blocking collectives, on_device(): lax.psum(partial_sums[0].astype(jnp.bfloat16), 'ctx').astype(jnp.float32)  40.9 us
    all_gather x1, waiting for transfers between devices, on_device(): lax.all_gather(up_weight, 'shard', axis=0, tiled=True)  32.7 us
    all_gather x2, blocking collectives, joined(): everything = jax.tree.map(lambda part: lax.all_gather(part, axis), x)  30.9 us
  transfers between devices with their start and end apart: 22, of which 18 were waited for; matrix products, arithmetic and copies ran while one was open for 19% of the time, Pallas kernels for 0%

commit v1 on v0

v1 whole, which is shorter than its diff:
```python
import jax
import jax.numpy as jnp
from jax import lax
from jax.experimental import pallas as pl
from jax.experimental.pallas import tpu as pltpu
from jax.sharding import PartitionSpec as P

HEAD_DIM = 64
RING = 4
CORES = 2
GROUP_HEADS = 3
GROUP_WIDTH = GROUP_HEADS * HEAD_DIM
WIDE = 256
BLOCK = 256

norm_eps = 1e-05
lowest = -1e30
tiny = 1e-30
log2_e = 1.4426950408889634
ln_2 = 0.6931471805599453

bf16 = jnp.bfloat16
f32 = jnp.float32


def norm_rows(values, gain, shift):
    center = values - jnp.mean(values, axis=-1, keepdims=True)
    spread = jnp.mean(center * center, axis=-1, keepdims=True)
    return center * lax.rsqrt(spread + norm_eps) * gain + shift


def dense(left, right):
    return jnp.dot(left, right, preferred_element_type=f32)


def contract_rows(left, right):
    return lax.dot_general(left, right, (((0,), (0,)), ((), ())), preferred_element_type=f32)


def contract_cols(left, right):
    return lax.dot_general(left, right, (((1,), (1,)), ((), ())), preferred_element_type=f32)


def move_z(x, hops):
    size = RING * CORES
    return lax.ppermute(x, "shard", [(r, (r + CORES * hops) % size) for r in range(size)])


def swap_core(x):
    return lax.ppermute(x, "shard", [(r, r ^ 1) for r in range(RING * CORES)])


def move_x(x, hops):
    pairs = [(c, (c // RING) * RING + (c + hops) % RING) for c in range(RING * RING)]
    return lax.ppermute(x, "ctx", pairs)


def move_y(x, hops):
    size = RING * RING
    return lax.ppermute(x, "ctx", [(c, (c + RING * hops) % size) for c in range(size)])


def pick(x, at):
    return lax.dynamic_index_in_dim(x, at % RING, 0, keepdims=False)


def in_order(parts, mine):
    around = jnp.stack([parts[0], parts[3], parts[2], parts[1], parts[0], parts[3], parts[2]])
    return lax.dynamic_slice_in_dim(around, (RING - mine) % RING, RING, 0)


def spread(x, move):
    return [x] + [move(x, k) for k in range(1, RING)]


def exchange(chunks, mine, move):
    return [pick(chunks, mine)] + [move(pick(chunks, mine + k), k) for k in range(1, RING)]


def sum_parts(parts):
    total = parts[0].astype(f32)
    for part in parts[1:]:
        total = total + part.astype(f32)
    return total


def sum_over_ctx(x, y, xq):
    rows, cols = x.shape
    share = sum_parts(exchange(x.reshape(RING, rows // RING, cols), xq, move_x)).astype(bf16)
    share = share.reshape(RING, rows // RING // RING, cols)
    part = sum_parts(exchange(share, y, move_y)).astype(bf16)
    share = in_order(spread(part, move_y), y).reshape(rows // RING, cols)
    return in_order(spread(share, move_x), xq).reshape(rows, cols)


def nt(left, right):
    return lax.dot_general(left, right, (((1,), (1,)), ((), ())), preferred_element_type=f32)


def places(parity, rows, own_first):
    at = rows % BLOCK
    side = jnp.where(rows < BLOCK, parity, 1 - parity) if own_first else parity
    return (at // 128) * 256 + side * 128 + at % 128


def allowed_block(parity):
    key_at = lax.broadcasted_iota(jnp.int32, (BLOCK, 2 * BLOCK), 0)
    query_at = lax.broadcasted_iota(jnp.int32, (BLOCK, 2 * BLOCK), 1)
    return places(parity, key_at, False) <= places(parity, query_at, True)


def split3(value):
    high = value.astype(bf16).astype(f32)
    rest = value - high
    mid = rest.astype(bf16).astype(f32)
    return high, mid, rest - mid


def lanes_of(rows, first, last):
    lane = lax.broadcasted_iota(jnp.int32, (rows, WIDE), 1)
    return jnp.where((lane >= first) & (lane < last), 1.0, 0.0).astype(bf16)


def forward_kernel(meta, q_own, q_oth, kv, o_own, o_oth, k_head, v_turned, best, total, acc):
    parity = meta[16]
    for h in range(GROUP_HEADS):
        mask = lanes_of(BLOCK, HEAD_DIM * h, HEAD_DIM * (h + 1))
        for j in range(8):
            k_head[j, BLOCK * h : BLOCK * (h + 1), :] = kv[j, :, :WIDE] * mask
    for j in range(8):
        v_turned[j] = kv[j, :, 128:].astype(f32).T.astype(bf16)

    def one_span(i, carry):
        best[...] = jnp.full(best.shape, lowest, f32)
        total[...] = jnp.zeros(total.shape, f32)
        acc[...] = jnp.zeros(acc.shape, f32)

        def visit(j, masked):
            query = jnp.concatenate([q_own[i], q_oth[i]], axis=0)
            if masked:
                allowed = allowed_block(parity)
            for h in range(GROUP_HEADS):
                scores = nt(k_head[j, BLOCK * h : BLOCK * (h + 1), :], query)
                if masked:
                    scores = jnp.where(allowed, scores, lowest)
                old = best[h : h + 1, :]
                new = jnp.maximum(old, jnp.max(scores, axis=0, keepdims=True))
                weights = jnp.exp2(scores - new)
                if masked:
                    weights = jnp.where(allowed, weights, 0.0)
                fade = jnp.exp2(old - new)
                best[h : h + 1, :] = new
                total[h : h + 1, :] = total[h : h + 1, :] * fade + jnp.sum(
                    weights, axis=0, keepdims=True
                )
                here = slice(HEAD_DIM * h, HEAD_DIM * (h + 1))
                values = v_turned[j, HEAD_DIM * (h + 1) : HEAD_DIM * (h + 2), :]
                acc[here, :] = acc[here, :] * fade + dense(values, weights.astype(bf16))

        def one_block(j, carry):
            @pl.when(meta[8 + j] < meta[i])
            def _():
                visit(j, False)

            @pl.when(meta[8 + j] == meta[i])
            def _():
                visit(j, True)

            return carry

        lax.fori_loop(0, 8, one_block, 0)
        row = lax.broadcasted_iota(jnp.int32, (HEAD_DIM, 2 * BLOCK), 0)
        pieces = []
        extra = jnp.zeros((HEAD_DIM, 2 * BLOCK), f32)
        for h in range(GROUP_HEADS):
            count = jnp.maximum(total[h : h + 1, :], tiny)
            pieces.append(acc[HEAD_DIM * h : HEAD_DIM * (h + 1), :] / count)
            terms = split3(best[h : h + 1, :] + jnp.log(count) * log2_e)
            for t in range(3):
                extra = jnp.where(row == 3 * h + t, terms[t], extra)
        turned = jnp.concatenate(pieces + [extra], axis=0).T.astype(bf16)
        o_own[i] = turned[:BLOCK]
        o_oth[i] = turned[BLOCK:]
        return carry

    lax.fori_loop(0, 8, one_span, 0)


def forward_call(meta, q_own, q_oth, kv):
    vmem = pl.BlockSpec(memory_space=pltpu.VMEM)
    shape = jax.ShapeDtypeStruct((8, BLOCK, WIDE), bf16)
    return pl.pallas_call(
        forward_kernel,
        out_shape=(shape, shape),
        in_specs=[pl.BlockSpec(memory_space=pltpu.SMEM), vmem, vmem, vmem],
        out_specs=(vmem, vmem),
        scratch_shapes=[
            pltpu.VMEM((8, GROUP_HEADS * BLOCK, WIDE), bf16),
            pltpu.VMEM((8, WIDE, BLOCK), bf16),
            pltpu.VMEM((8, 2 * BLOCK), f32),
            pltpu.VMEM((8, 2 * BLOCK), f32),
            pltpu.VMEM((GROUP_WIDTH, 2 * BLOCK), f32),
        ],
        compiler_params=pltpu.CompilerParams(vmem_limit_bytes=50 * 2**20),
        name="attention_forward",
    )(meta, q_own, q_oth, kv)


def merge_kernel(*refs):
    ins, out = refs[:-1], refs[-1]
    row = lax.broadcasted_iota(jnp.int32, (WIDE, WIDE), 0)
    col = lax.broadcasted_iota(jnp.int32, (WIDE, WIDE), 1)

    def ones_at(where):
        return jnp.where(where, 1.0, 0.0).astype(bf16)

    to_lanes = ones_at((row >= 192) & (row < 201) & (col < 192) & ((row - 192) // 3 == col // 64))
    logs = [dense(x[...], to_lanes) for x in ins]
    best = logs[0]
    for part in logs[1:]:
        best = jnp.maximum(best, part)
    total = jnp.zeros_like(best)
    context = jnp.zeros_like(best)
    for x, part in zip(ins, logs):
        weight = jnp.exp2(part - best)
        total = total + weight
        context = context + weight * x[...].astype(f32)
    context = context / total
    terms = split3(best + jnp.log(total) * log2_e)
    extra = jnp.zeros_like(best)
    for t in range(3):
        back = ones_at((row < 192) & (row % 64 == 0) & (col == 192 + 3 * (row // 64) + t))
        extra = extra + dense(terms[t].astype(bf16), back)
    lane = lax.broadcasted_iota(jnp.int32, best.shape, 1)
    out[...] = jnp.where(lane < 192, context, extra).astype(bf16)


def merge_call(parts):
    rows = parts[0].shape[0]
    block = 512
    spec = pl.BlockSpec((block, WIDE), lambda i: (i, 0))
    return pl.pallas_call(
        merge_kernel,
        out_shape=jax.ShapeDtypeStruct((rows, WIDE), bf16),
        grid=(rows // block,),
        in_specs=[spec] * len(parts),
        out_specs=spec,
        compiler_params=pltpu.CompilerParams(vmem_limit_bytes=50 * 2**20),
        name="merge_partial_attention",
    )(*parts)


def pack_kernel(dcontext, context, out):
    row = lax.broadcasted_iota(jnp.int32, (GROUP_WIDTH, WIDE), 0)
    col = lax.broadcasted_iota(jnp.int32, (GROUP_WIDTH, WIDE), 1)

    def ones_at(where):
        return jnp.where(where, 1.0, 0.0).astype(bf16)

    product = dcontext[...].astype(f32) * context[:, :GROUP_WIDTH].astype(f32)
    by_head = ones_at((col < 9) & (row // 64 == col // 3))
    delta = jnp.zeros(out.shape, f32)
    for term in split3(product):
        delta = delta + dense(term.astype(bf16), by_head)
    high, mid, low = split3(delta)
    lane = lax.broadcasted_iota(jnp.int32, out.shape, 1)
    delta_terms = jnp.where(lane % 3 == 0, high, jnp.where(lane % 3 == 1, mid, low))
    row2 = lax.broadcasted_iota(jnp.int32, (WIDE, WIDE), 0)
    col2 = lax.broadcasted_iota(jnp.int32, (WIDE, WIDE), 1)
    log_terms = dense(
        context[...], ones_at((row2 >= 192) & (row2 < 201) & (col2 == row2 - 183))
    )
    shifted = dense(dcontext[...], ones_at(col == row + 64))
    out[...] = jnp.where(
        lane < 9, -delta_terms, jnp.where(lane < 18, -log_terms, shifted)
    ).astype(bf16)


def pack_call(dcontext, context):
    return pl.pallas_call(
        pack_kernel,
        out_shape=jax.ShapeDtypeStruct(context.shape, bf16),
        compiler_params=pltpu.CompilerParams(vmem_limit_bytes=50 * 2**20),
        name="pack_context_gradient",
    )(dcontext, context)


def backward_kernel(
    meta,
    q_own,
    q_oth,
    d_own,
    d_oth,
    kv,
    dq_own,
    dq_oth,
    dkv,
    k_head,
    v_head,
    k_turned,
    q_full,
    d_full,
    q_head,
    d_head,
    dq_acc,
    dk_acc,
    dv_acc,
):
    parity = meta[16]
    lane = lax.broadcasted_iota(jnp.int32, (BLOCK, 128), 1)

    def prepare_queries(i, carry):
        for side, (q_ref, d_ref) in enumerate(((q_own, d_own), (q_oth, d_oth))):
            rows = slice(BLOCK * side, BLOCK * (side + 1))
            query, grad = q_ref[i], d_ref[i]
            d_full[i, rows, :] = grad
            q_full[i, rows, :128] = query[:, :128]
            logs = pltpu.roll(grad[:, :128].astype(f32), 64, 1)
            q_full[i, rows, 128:] = jnp.where(
                lane < 64, query[:, 128:].astype(f32), logs
            ).astype(bf16)
            for h in range(GROUP_HEADS):
                there = slice(2 * BLOCK * h + BLOCK * side, 2 * BLOCK * h + BLOCK * (side + 1))
                q_head[i, there, :] = query * lanes_of(BLOCK, HEAD_DIM * h, HEAD_DIM * (h + 1))
                d_head[i, there, :] = grad * lanes_of(
                    BLOCK, HEAD_DIM * (h + 1), HEAD_DIM * (h + 2)
                )
        dq_acc[i] = jnp.zeros(dq_acc.shape[1:], f32)
        return carry

    lax.fori_loop(0, 8, prepare_queries, 0)

    def prepare_keys(j, carry):
        keys = kv[j, :, :WIDE]
        values = kv[j, :, 128:]
        for h in range(GROUP_HEADS):
            there = slice(BLOCK * h, BLOCK * (h + 1))
            k_head[j, there, :] = keys * lanes_of(
                BLOCK, HEAD_DIM * h, HEAD_DIM * (h + 1)
            ) + lanes_of(BLOCK, 201 + 3 * h, 204 + 3 * h)
            v_head[j, there, :] = values * lanes_of(
                BLOCK, HEAD_DIM * (h + 1), HEAD_DIM * (h + 2)
            ) + lanes_of(BLOCK, 3 * h, 3 * h + 3)
        k_turned[j] = keys.astype(f32).T.astype(bf16)
        return carry

    lax.fori_loop(0, 8, prepare_keys, 0)

    def one_key_block(j, carry):
        dk_acc[...] = jnp.zeros(dk_acc.shape, f32)
        dv_acc[...] = jnp.zeros(dv_acc.shape, f32)

        def visit(i, masked):
            if masked:
                allowed = allowed_block(parity)
            query = q_full[i]
            grad = d_full[i]
            all_weights = []
            all_dscores = []
            for h in range(GROUP_HEADS):
                there = slice(BLOCK * h, BLOCK * (h + 1))
                weights = jnp.exp2(nt(k_head[j, there, :], query))
                if masked:
                    weights = jnp.where(allowed, weights, 0.0)
                dscores = (weights * nt(v_head[j, there, :], grad)).astype(bf16)
                here = slice(HEAD_DIM * h, HEAD_DIM * (h + 1))
                dq_acc[i, here, :] = dq_acc[i, here, :] + dense(k_turned[j, here, :], dscores)
                all_weights.append(weights.astype(bf16))
                all_dscores.append(dscores)
            dv_acc[...] = dv_acc[...] + dense(jnp.concatenate(all_weights, axis=1), d_head[i])
            dk_acc[...] = dk_acc[...] + dense(jnp.concatenate(all_dscores, axis=1), q_head[i])

        def one_span(i, carry):
            @pl.when(meta[8 + j] < meta[i])
            def _():
                visit(i, False)

            @pl.when(meta[8 + j] == meta[i])
            def _():
                visit(i, True)

            return carry

        lax.fori_loop(0, 8, one_span, 0)
        dk = dk_acc[...] * ln_2
        dv = dv_acc[...]
        dkv[j, :, :128] = dk[:, :128].astype(bf16)
        dkv[j, :, 128:256] = jnp.where(lane < 64, dk[:, 128:], dv[:, :128]).astype(bf16)
        dkv[j, :, 256:] = dv[:, 128:].astype(bf16)
        return carry

    lax.fori_loop(0, 8, one_key_block, 0)

    def finish(i, carry):
        filled = jnp.concatenate(
            [dq_acc[i], jnp.zeros((WIDE - GROUP_WIDTH, 2 * BLOCK), f32)], axis=0
        )
        turned = filled.T.astype(bf16)
        dq_own[i] = turned[:BLOCK]
        dq_oth[i] = turned[BLOCK:]
        return carry

    lax.fori_loop(0, 8, finish, 0)


def backward_call(meta, q_own, q_oth, d_own, d_oth, kv):
    vmem = pl.BlockSpec(memory_space=pltpu.VMEM)
    shape = jax.ShapeDtypeStruct((8, BLOCK, WIDE), bf16)
    heads = GROUP_HEADS
    return pl.pallas_call(
        backward_kernel,
        out_shape=(shape, shape, jax.ShapeDtypeStruct(kv.shape, bf16)),
        in_specs=[pl.BlockSpec(memory_space=pltpu.SMEM)] + [vmem] * 5,
        out_specs=(vmem, vmem, vmem),
        scratch_shapes=[
            pltpu.VMEM((8, heads * BLOCK, WIDE), bf16),
            pltpu.VMEM((8, heads * BLOCK, WIDE), bf16),
            pltpu.VMEM((8, WIDE, BLOCK), bf16),
            pltpu.VMEM((8, 2 * BLOCK, WIDE), bf16),
            pltpu.VMEM((8, 2 * BLOCK, WIDE), bf16),
            pltpu.VMEM((8, heads * 2 * BLOCK, WIDE), bf16),
            pltpu.VMEM((8, heads * 2 * BLOCK, WIDE), bf16),
            pltpu.VMEM((8, GROUP_WIDTH, 2 * BLOCK), f32),
            pltpu.VMEM((BLOCK, WIDE), f32),
            pltpu.VMEM((BLOCK, WIDE), f32),
        ],
        compiler_params=pltpu.CompilerParams(vmem_limit_bytes=56 * 2**20),
        name="attention_backward",
    )(meta, q_own, q_oth, d_own, d_oth, kv)


def on_device(
    tokens,
    span_order,
    first_gain,
    first_shift,
    query_weight,
    query_bias,
    key_weight,
    value_weight,
    value_bias,
    out_weight,
    out_bias,
    second_gain,
    second_shift,
    up_weight,
    up_bias,
    down_weight,
    down_bias,
    cotangent,
):
    shard_at = lax.axis_index("shard")
    z, core = shard_at // CORES, shard_at % CORES
    ctx_at = lax.axis_index("ctx")
    y, xq = ctx_at // RING, ctx_at % RING
    rows, width = tokens.shape
    ranks = RING * CORES
    hidden_width = up_weight.shape[1]
    part_rows = width // ranks

    steps = jnp.arange(RING, dtype=jnp.int32)
    groups = jnp.concatenate([((y - steps) % RING) * RING + xq, y * RING + (xq - steps) % RING])
    stored = (2 * groups[:, None] + jnp.arange(2, dtype=jnp.int32)[None, :]).reshape(-1)
    found = stored[:, None] == jnp.arange(span_order.shape[0], dtype=jnp.int32)[None, :]
    spans = jnp.sum(jnp.where(found, span_order[None, :], 0), axis=1)
    meta = jnp.concatenate([spans, core[None].astype(jnp.int32)])

    vectors = jnp.concatenate(
        [
            first_gain,
            first_shift,
            query_bias,
            value_bias,
            out_bias,
            second_gain,
            second_shift,
            down_bias,
            up_bias,
        ]
    ).reshape(2, 3 * GROUP_WIDTH)
    by_place = jnp.concatenate(
        [w.reshape(part_rows, RING, GROUP_WIDTH) for w in (query_weight, key_weight, value_weight)],
        axis=2,
    ).transpose(1, 0, 2)
    sent = jnp.concatenate(
        [by_place, jnp.broadcast_to(vectors[None], (RING,) + vectors.shape)], axis=1
    )
    token_parts = spread(tokens, move_z)
    own_part = in_order(exchange(sent, z, move_z), z)
    other_part = swap_core(own_part)
    first_core = jnp.where(core == 0, own_part, other_part)
    second_core = jnp.where(core == 0, other_part, own_part)
    joined = jnp.stack([first_core, second_core], axis=1)
    w_qkv = joined[:, :, :part_rows].reshape(width, 3 * GROUP_WIDTH)
    vec = joined[:, :, part_rows:].reshape(ranks, -1)

    def vector(k):
        return vec[:, part_rows * k : part_rows * (k + 1)].reshape(-1).astype(f32)

    gain_one, shift_one, b_query, b_value, b_out, gain_two, shift_two, b_down = (
        vector(k) for k in range(8)
    )
    b_up = vec[:, 8 * part_rows :].reshape(-1).astype(f32)

    w_out = lax.all_gather(out_weight, "shard", axis=0, tiled=True)
    w_up = lax.all_gather(up_weight, "shard", axis=0, tiled=True)
    w_down = lax.all_gather(down_weight, "shard", axis=0, tiled=True)

    span_tokens = in_order(token_parts, z).reshape(RING * rows, width)
    normed_low = norm_rows(span_tokens.astype(f32), gain_one, shift_one).astype(bf16)
    projected = dense(normed_low, w_qkv)
    my_cols = GROUP_WIDTH * z
    bias_q = lax.dynamic_slice_in_dim(b_query, my_cols, GROUP_WIDTH)
    bias_v = lax.dynamic_slice_in_dim(b_value, my_cols, GROUP_WIDTH)
    queries = ((projected[:, :GROUP_WIDTH] + bias_q) * (0.125 * log2_e)).astype(bf16)
    queries = jnp.pad(queries, ((0, 0), (0, WIDE - GROUP_WIDTH)))
    kv_own = jnp.concatenate(
        [
            projected[:, GROUP_WIDTH : 2 * GROUP_WIDTH],
            projected[:, 2 * GROUP_WIDTH :] + bias_v,
        ],
        axis=1,
    ).astype(bf16)

    q_own = jnp.stack(spread(queries, move_y))
    kv_all = jnp.stack(spread(kv_own, move_x))
    q_oth = swap_core(q_own)
    q_own = q_own.reshape(8, BLOCK, WIDE)
    q_oth = q_oth.reshape(8, BLOCK, WIDE)
    kv_all = kv_all.reshape(8, BLOCK, 2 * GROUP_WIDTH)
    out_own, out_oth = forward_call(meta, q_own, q_oth, kv_all)

    swapped = swap_core(out_oth)
    merged = merge_call(
        [out_own.reshape(-1, WIDE), swapped.reshape(-1, WIDE)]
    ).reshape(RING, RING * rows, WIDE)
    context_packed = merge_call([merged[0]] + [move_y(merged[k], -k) for k in range(1, RING)])
    by_token = jnp.stack(
        [merged_part for merged_part in exchange(
            context_packed[:, :GROUP_WIDTH].reshape(RING, rows, GROUP_WIDTH), z, move_z
        )]
    )
    context_low = (
        in_order([by_token[k] for k in range(RING)], z).transpose(1, 0, 2).reshape(rows, width)
    )

    tokens_f = tokens.astype(f32)
    middle = tokens_f + dense(context_low, w_out) + b_out
    second, second_back = jax.vjp(norm_rows, middle, gain_two, shift_two)
    second_low = second.astype(bf16)
    pre_act = dense(second_low, w_up) + b_up
    hidden, gelu_back = jax.vjp(jax.nn.gelu, pre_act)
    hidden_low = hidden.astype(bf16)
    activations = (middle + dense(hidden_low, w_down) + b_down).astype(bf16)
    upstream = cotangent.astype(f32)
    grad_down_bias = jnp.sum(upstream, axis=0)
    dpre = gelu_back(contract_cols(cotangent, w_down))[0].astype(bf16)
    grad_up_bias = jnp.sum(dpre.astype(f32), axis=0)
    dmid_norm, grad_second_gain, grad_second_shift = second_back(contract_cols(dpre, w_up))
    dmiddle = upstream + dmid_norm
    dmid_low = dmiddle.astype(bf16)
    grad_out_bias = jnp.sum(dmid_low.astype(f32), axis=0)
    dcontext = contract_cols(dmid_low, w_out).astype(bf16)

    dcontext_mine = in_order(
        exchange(dcontext.reshape(rows, RING, GROUP_WIDTH).transpose(1, 0, 2), z, move_z), z
    ).reshape(RING * rows, GROUP_WIDTH)
    packed = pack_call(dcontext_mine, context_packed)
    d_own = jnp.stack(spread(packed, move_y))
    d_oth = swap_core(d_own)
    dq_own, dq_oth, dkv = backward_call(
        meta,
        q_own,
        q_oth,
        d_own.reshape(8, BLOCK, WIDE),
        d_oth.reshape(8, BLOCK, WIDE),
        kv_all,
    )

    def columns(x):
        return x.reshape(rows, RING, -1).transpose(1, 0, 2)

    def tokens_joined(parts):
        return in_order(parts, z).reshape(RING * rows, -1)

    cot_z = tokens_joined(spread(cotangent, move_z))
    hidden_z = tokens_joined(exchange(columns(hidden_low), z, move_z))
    second_z = tokens_joined(exchange(columns(second_low), z, move_z))
    dpre_z = tokens_joined(spread(dpre, move_z))
    dmid_z = tokens_joined(spread(dmid_low, move_z))
    grad_down = contract_rows(hidden_z, cot_z)
    grad_up = contract_rows(second_z, dpre_z)
    grad_out = contract_rows(context_packed[:, :GROUP_WIDTH], dmid_z)

    def core_half(x, at):
        half = x.shape[0] // CORES
        return lax.dynamic_slice_in_dim(x, at * half, half, 0)

    def rank_rows(at):
        up = core_half(grad_up, at)
        return jnp.concatenate(
            [core_half(grad_down, at), core_half(grad_out, at)]
            + [up[:, width * k : width * (k + 1)] for k in range(hidden_width // width)],
            axis=0,
        )

    early = rank_rows(core) + swap_core(rank_rows(1 - core).astype(bf16)).astype(f32)
    early = jnp.pad(early.astype(bf16), ((0, 32), (0, 0)))
    early = sum_over_ctx(early, y, xq).astype(f32)
    grad_down_weight = early[: 4 * part_rows]
    grad_out_weight = early[4 * part_rows : 5 * part_rows]
    grad_up_weight = jnp.concatenate(
        [early[(5 + k) * part_rows : (6 + k) * part_rows] for k in range(hidden_width // width)],
        axis=1,
    )

    dq_mine = dq_own.astype(f32) + swap_core(dq_oth).astype(f32)
    dq_mine = dq_mine.astype(bf16).reshape(RING, RING * rows, WIDE)
    dq_sum = sum_parts([dq_mine[0]] + [move_y(dq_mine[k], -k) for k in range(1, RING)])
    dkv_parts = dkv.reshape(RING, RING * rows, 2 * GROUP_WIDTH)
    dkv_sum = sum_parts([dkv_parts[0]] + [move_x(dkv_parts[k], -k) for k in range(1, RING)])
    dq_low = dq_sum[:, :GROUP_WIDTH].astype(bf16) * bf16(0.125)
    dqkv = jnp.concatenate([dq_low, dkv_sum.astype(bf16)], axis=1)
    grad_qkv = contract_rows(normed_low, dqkv).astype(bf16)
    bias_grads = jnp.sum(dqkv.astype(f32), axis=0)

    dnormed_part = contract_cols(dqkv, w_qkv).astype(bf16).reshape(RING, rows, width)
    dnormed = sum_parts(exchange(dnormed_part, z, move_z))
    _, first_back = jax.vjp(norm_rows, tokens_f, gain_one, shift_one)
    dtok_norm, grad_first_gain, grad_first_shift = first_back(dnormed)
    input_grad = dmiddle + dtok_norm

    def placed(x):
        return lax.dynamic_update_slice(jnp.zeros((width,), f32), x, (my_cols,))

    vec_grads = jnp.concatenate(
        [
            v.reshape(ranks, -1)
            for v in (
                grad_first_gain,
                grad_first_shift,
                placed(bias_grads[:GROUP_WIDTH]),
                placed(bias_grads[2 * GROUP_WIDTH :]),
                grad_out_bias,
                grad_second_gain,
                grad_second_shift,
                grad_down_bias,
                grad_up_bias,
            )
        ],
        axis=1,
    )
    vec_rows = vec_grads.astype(bf16).reshape(RING, CORES * 2, 3 * GROUP_WIDTH)
    weight_rows = grad_qkv.reshape(RING, CORES * part_rows, 3 * GROUP_WIDTH)
    late_parts = exchange(jnp.concatenate([weight_rows, vec_rows], axis=1), z, move_z)
    weight_cols = in_order(late_parts, z)[:, : CORES * part_rows].reshape(
        RING, CORES, part_rows, 3 * GROUP_WIDTH
    )
    vec_sum = sum_parts([part[CORES * part_rows :] for part in late_parts]).reshape(
        CORES, 2, 3 * GROUP_WIDTH
    )

    def late_rows(at):
        mine = lax.dynamic_index_in_dim(weight_cols, at, 1, keepdims=False)
        return jnp.concatenate(
            [
                mine.reshape(RING * part_rows, 3 * GROUP_WIDTH),
                lax.dynamic_index_in_dim(vec_sum, at, 0, keepdims=False).astype(bf16),
            ],
            axis=0,
        )

    late = late_rows(core).astype(f32) + swap_core(late_rows(1 - core)).astype(f32)
    late = jnp.pad(late.astype(bf16), ((0, 512 - late.shape[0]), (0, 0)))
    late = sum_over_ctx(late, y, xq).astype(f32)
    late_weights = late[: RING * part_rows].reshape(RING, part_rows, 3, GROUP_WIDTH)
    late_weights = late_weights.transpose(2, 1, 0, 3).reshape(3, part_rows, width)
    late_vec = late[RING * part_rows : RING * part_rows + 2].reshape(-1)

    def late_vector(k):
        return late_vec[part_rows * k : part_rows * (k + 1)]

    return (
        activations,
        input_grad,
        late_vector(0),
        late_vector(1),
        late_weights[0],
        late_vector(2),
        late_weights[1],
        late_weights[2],
        late_vector(3),
        grad_out_weight,
        late_vector(4),
        late_vector(5),
        late_vector(6),
        grad_up_weight,
        late_vec[8 * part_rows :],
        grad_down_weight,
        late_vector(7),
    )


def solution(mesh):
    tokens_spec = P(("ctx", "shard"), None)
    vector_spec = P("shard")
    matrix_spec = P("shard", None)
    return jax.shard_map(
        on_device,
        mesh=mesh,
        in_specs=(
            tokens_spec,
            P(),
            vector_spec,
            vector_spec,
            matrix_spec,
            vector_spec,
            matrix_spec,
            matrix_spec,
            vector_spec,
            matrix_spec,
            vector_spec,
            vector_spec,
            vector_spec,
            matrix_spec,
            vector_spec,
            matrix_spec,
            vector_spec,
            tokens_spec,
        ),
        out_specs=(
            tokens_spec,
            tokens_spec,
            vector_spec,
            vector_spec,
            matrix_spec,
            vector_spec,
            matrix_spec,
            matrix_spec,
            vector_spec,
            matrix_spec,
            vector_spec,
            vector_spec,
            vector_spec,
            matrix_spec,
            vector_spec,
            matrix_spec,
            vector_spec,
        ),
        check_vma=False,
    )
```

time: 1340 us -> 572 us (0.43)
  waiting for transfers between devices: 654 us -> 188 us
  matrix products: 226 us -> 23.3 us
  blocking collectives: 155 us -> 0 us
  Pallas kernels: 0 us -> 115 us
  starting transfers between devices: 1.36 us -> 87.2 us
  other arithmetic: 98.2 us -> 30.3 us
  loops' own time: 65.2 us -> 0 us
  local copies, waits for them, and re-layouts: 123 us -> 102 us
    unnamed x26 -> x3, waiting for transfers between devices: 261 us -> 1.39 us
    reduce_scatter x7 -> x0, waiting for transfers between devices: 233 us -> none  [the longest x6 210 us: on_device(): lax.psum_scatter(as_sent((grad_first_gain, grad_first_shift, contract_row...]
    ppermute x0 -> x82, waiting for transfers between devices: none -> 187 us  [the longest x33 77.6 us: move_z(): lax.ppermute(x, 'shard', [(r, (r + CORES * hops) % size) for r in range(s...]
    dot_general x87 -> x4, matrix products: 194 us -> 9.12 us  [dense(): return jnp.dot(left, right, preferred_element_type=f32)]
    all_gather x10 -> x3, waiting for transfers between devices: 147 us -> 0.04 us  [the longest x1 0.02 us: on_device(): w_up = lax.all_gather(up_weight, 'shard', axis=0, tiled=True)]
    pallas_call x0 -> x5, Pallas kernels: none -> 115 us  [the longest x1 63.6 us: backward_call(): pl.pallas_call(backward_kernel, out_shape=(shape, shape, jax.ShapeDtypeSt...]
    ppermute x0 -> x82, starting transfers between devices: none -> 87.1 us  [the longest x33 42.5 us: move_z(): lax.ppermute(x, 'shard', [(r, (r + CORES * hops) % size) for r in range(s...]
    another operation x58 -> x0, loops' own time: 65.2 us -> none  [the longest x2 21.2 us: block_stats(): finished, unused = lax.scan(visit, initial, (key_split, key_marks))]
  transfers between devices with their start and end apart: 22 -> 85, of which waited for: 18 -> 51; matrix products, arithmetic and copies ran while one was open for 19% -> 24% of each run, Pallas kernels for 0% -> 20%
where the time goes in v1:
time: 572 us; the launch traced here: 562 us
  waiting for transfers between devices  188 us (33%)
  Pallas kernels  115 us (20%)
  local copies, waits for them, and re-layouts  102 us (18%)
  starting transfers between devices  87.2 us (15%)
  other arithmetic  30.3 us (5%)
  matrix products  23.3 us (4%)
  between operations  16 us (3%)
    ppermute x33, waiting for transfers between devices, move_z(): lax.ppermute(x, 'shard', [(r, (r + CORES * hops) % size) for r in range(s...  77.6 us
    pallas_call x1, Pallas kernels, backward_call(): pl.pallas_call(backward_kernel, out_shape=(shape, shape, jax.ShapeDtypeSt...  63.6 us
    ppermute x18, waiting for transfers between devices, move_x(): return lax.ppermute(x, 'ctx', pairs)  61.4 us
    ppermute x24, waiting for transfers between devices, move_y(): lax.ppermute(x, 'ctx', [(c, (c + RING * hops) % size) for c in range(size)])  47.9 us
    pallas_call x1, Pallas kernels, forward_call(): pl.pallas_call(forward_kernel, out_shape=(shape, shape), in_specs=[pl.Blo...  45.5 us
    unnamed x188, local copies, waits for them, and re-layouts  42.6 us
    ppermute x33, starting transfers between devices, move_z(): lax.ppermute(x, 'shard', [(r, (r + CORES * hops) % size) for r in range(s...  42.5 us
    ppermute x24, starting transfers between devices, move_y(): lax.ppermute(x, 'ctx', [(c, (c + RING * hops) % size) for c in range(size)])  26.3 us
  transfers between devices with their start and end apart: 85, of which 51 were waited for; matrix products, arithmetic and copies ran while one was open for 24% of the time, Pallas kernels for 20%

profile of v1, /device:TPU:0, one launch (start us, length us, event | category | flops | bytes accessed | tf_op | source)
XLA Modules:
  0.0 562.2 jit_solution(11667514570803008502)
XLA Ops:
  8.7 4.2 collective-permute-start
  12.9 6.1 %concatenate.66 = bf16[1152]{0:T(1024)(128)(2,1)S(1)} concatenate(bf16[96]{0:T(256)(128)(2,1)} %param.20, bf16[96]{0:T(256)(128)(2,1)} %param.21, bf16[96]{0:T(256)(128)(2,1)} %param.23, bf16[96]{0:T(256)(128)(2,1)} %param.26, bf16[96]{0:T(256)(128)(2,1)} %param.28, bf16[96]{0:T(256)(128)(2,1)} %param.29, bf16[96]{0:T(256)(128)(2,1)} %param.30, bf16[96]{0:T(256)(128)(2,1)} %param.34, ...), dimensions={0} | concatenate | bytes 4608 | tf_op jit(solution)/shard_map/concatenate | solution.py:468
  24.1 3.0 collective-permute-start.4
  28.7 3.2 collective-permute-done.3
  34.5 2.7 collective-permute-done.5
  38.1 5.9 %stack.289 = bf16[7,98,576]{2,0,1:T(8,128)(2,1)S(1)} concatenate(bf16[1,98,576]{2,0,1:T(2,128)(2,1)S(1)} %get-tuple-element.91, bf16[1,98,576]{2,0,1:T(2,128)(2,1)S(1)} %copy.108, bf16[1,98,576]{2,0,1:T(2,128)(2,1)S(1)} %copy.109, bf16[1,98,576]{2,0,1:T(2,128)(2,1)} %copy.110, bf16[1,98,576]{2,0,1:T(2,128)(2,1)S(1)} %get-tuple-element.91, bf16[1,98,576]{2,0,1:T(2,128)(2,1)S(1)} %copy.108, ...), dimensions={0} | concatenate | bytes 1580544 | tf_op jit(solution)/shard_map/stack | solution.py:68
  56.4 2.9 collective-permute-start.9
  60.9 10.3 %collective-permute-done.9 = bf16[512,256]{0,1:T(8,128)(2,1)S(1)} collective-permute-done((bf16[512,256]{0,1:T(8,128)(2,1)S(1)}, bf16[512,256]{0,1:T(8,128)(2,1)S(1)}, u32[]{:S(2)}, u32[]{:S(2)}) %collective-permute-start.9) | collective-permute-done | bytes 262176 | tf_op jit(solution)/shard_map/ppermute | solution.py:60
  71.3 3.7 collective-permute-done.7
  78.0 3.0 collective-permute-start.13
  83.5 15.3 %collective-permute-done.13 = bf16[512,384]{0,1:T(8,128)(2,1)S(1)} collective-permute-done((bf16[512,384]{0,1:T(8,128)(2,1)}, bf16[512,384]{0,1:T(8,128)(2,1)S(1)}, u32[]{:S(2)}, u32[]{:S(2)}) %collective-permute-start.13) | collective-permute-done | bytes 393248 | tf_op jit(solution)/shard_map/ppermute | solution.py:55
  98.8 3.7 collective-permute-done.11
  102.5 2.4 pad_maximum_fusion
  104.9 2.6 copy.117
  109.8 45.5 %attention_forward.1 = (bf16[8,256,256]{2,1,0:T(8,128)(2,1)S(1)}, bf16[8,256,256]{2,1,0:T(8,128)(2,1)S(1)}) custom-call(s32[17]{0:T(128)S(1)} %pad_add_fusion.meta, bf16[8,256,256]{2,1,0:T(8,128)(2,1)S(1)} %bitcast.336, bf16[8,256,256]{2,1,0:T(8,128)(2,1)} %bitcast.345, bf16[8,256,384]{2,1,0:T(8,128)(2,1)} %bitcast.343), custom_call_target="tpu_custom_call" | custom-call | tf_op jit(solution)/shard_map/attention_forward/pallas_call | solution.py:192
  156.4 2.5 collective-permute-start.58
  160.2 3.1 collective-permute-done.57
  167.4 3.5 merge_partial_attention.2
  175.7 4.5 collective-permute-done.15.refs_1_
  182.4 2.8 collective-permute-done.17.refs_3_
  186.9 5.2 collective-permute-start.18
  193.8 4.0 collective-permute-done.19
  208.4 5.2 multiply_convert_fusion
  213.6 5.8 %bitcast_dynamic-update-slice_fusion.5 = (bf16[7,128,3072]{2,1,0:T(8,128)(2,1)}, bf16[128,3072]{1,0:T(8,128)(2,1)S(1)}) fusion(f32[128,3072]{1,0:T(8,128)} %get-tuple-element.140, bf16[128,768]{1,0:T(8,128)(2,1)S(1)} %copy-done.15, bf16[3072,768]{1,0:T(8,128)(2,1)} %all-gather.8.cloned.1.call-done), kind=kOutput, calls=%fused_computation.60 | convolution fusion | flops 611844096 | bytes 8060928 | tf_op jit(solution)/shard_map/dot_general | solution.py:41
  225.0 2.9 collective-permute-start.66
  232.5 2.6 constant_dynamic-slice_fusion.3
  242.7 5.8 %collective-permute-done.21 = bf16[128,192]{0,1:T(8,128)(2,1)S(1)} collective-permute-done((bf16[128,192]{0,1:T(8,128)(2,1)S(1)}, bf16[128,192]{0,1:T(8,128)(2,1)S(1)}, u32[]{:S(2)}, u32[]{:S(2)}) %collective-permute-start.21) | collective-permute-done | bytes 49184 | tf_op jit(solution)/shard_map/ppermute | solution.py:46
  250.9 3.4 collective-permute-done.22
  256.1 3.8 collective-permute-done.23
  267.9 7.9 %collective-permute-done.55 = bf16[128,768]{0,1:T(8,128)(2,1)S(1)} collective-permute-done((bf16[128,768]{0,1:T(8,128)(2,1)S(1)}, bf16[128,768]{0,1:T(8,128)(2,1)S(1)}, u32[]{:S(2)}, u32[]{:S(2)}) %collective-permute-start.55) | collective-permute-done | bytes 196640 | tf_op jit(solution)/shard_map/ppermute | solution.py:46
  276.7 13.7 %collective-permute-done.56 = bf16[128,768]{0,1:T(8,128)(2,1)S(1)} collective-permute-done((bf16[128,768]{0,1:T(8,128)(2,1)S(1)}, bf16[128,768]{0,1:T(8,128)(2,1)S(1)}, u32[]{:S(2)}, u32[]{:S(2)}) %collective-permute-start.56) | collective-permute-done | bytes 196640 | tf_op jit(solution)/shard_map/ppermute | solution.py:46
  306.1 2.4 collective-permute-done.67
  308.5 8.3 %collective-permute-done.68 = bf16[128,3072]{1,0:T(8,128)(2,1)S(1)} collective-permute-done((bf16[128,3072]{1,0:T(8,128)(2,1)S(1)}, bf16[128,3072]{1,0:T(8,128)(2,1)S(1)}, u32[]{:S(2)}, u32[]{:S(2)}) %collective-permute-start.68) | collective-permute-done | bytes 786464 | tf_op jit(solution)/shard_map/ppermute | solution.py:46
  327.2 63.6 %attention_backward.1 = (bf16[8,256,256]{2,1,0:T(8,128)(2,1)}, bf16[8,256,256]{2,1,0:T(8,128)(2,1)}, bf16[8,256,384]{2,1,0:T(8,128)(2,1)}) custom-call(s32[17]{0:T(128)} %copy-done.1, bf16[8,256,256]{2,1,0:T(8,128)(2,1)} %bitcast.337, bf16[8,256,256]{2,1,0:T(8,128)(2,1)} %bitcast.346, bf16[8,256,256]{2,1,0:T(8,128)(2,1)} %bitcast.49.d_own, ...), custom_call_target="tpu_custom_call" | custom-call | tf_op jit(solution)/shard_map/attention_backward/pallas_call | solution.py:410
  390.8 2.4 fusion.94
  400.2 14.1 %collective-permute-done.34 = bf16[512,384]{1,0:T(8,128)(2,1)S(1)} collective-permute-done((bf16[512,384]{1,0:T(8,128)(2,1)S(1)}, bf16[512,384]{1,0:T(8,128)(2,1)S(1)}, u32[]{:S(2)}, u32[]{:S(2)}) %collective-permute-start.34) | collective-permute-done | bytes 393248 | tf_op jit(solution)/shard_map/ppermute | solution.py:55
  419.4 3.9 collective-permute-done.72
  423.3 3.8 collective-permute-done.71
  427.1 5.8 %collective-permute-done.70 = bf16[224,768]{1,0:T(8,128)(2,1)} collective-permute-done((bf16[224,768]{1,0:T(8,128)(2,1)}, bf16[224,768]{1,0:T(8,128)(2,1)}, u32[]{:S(2)}, u32[]{:S(2)}) %collective-permute-start.70) | collective-permute-done | bytes 344096 | tf_op jit(solution)/shard_map/ppermute | solution.py:55
  451.7 10.1 %collective-permute-done.77 = bf16[56,768]{1,0:T(8,128)(2,1)S(1)} collective-permute-done((bf16[56,768]{1,0:T(8,128)(2,1)S(1)}, bf16[56,768]{1,0:T(8,128)(2,1)S(1)}, u32[]{:S(2)}, u32[]{:S(2)}) %collective-permute-start.77) | collective-permute-done | bytes 86048 | tf_op jit(solution)/shard_map/ppermute | solution.py:60
  487.0 4.4 collective-permute-done.38
  493.2 2.7 collective-permute-done.40
  505.5 3.8 collective-permute-start.44
  512.4 4.5 collective-permute-done.44
  517.9 2.5 collective-permute-done.42
  524.5 2.6 collective-permute-done.46
  531.8 3.9 collective-permute-done.49
  541.8 4.7 collective-permute-done.52
  (508 shorter events, 211.6 us)
Async XLA Ops:
  7.2 191.3 %all-gather.4.cloned.1.call-start = ((), (), s32[]{:S(2)}) async-start(), calls=%async_computation | async-start | bytes 1327104 | tf_op jit(solution)/shard_map/all_gather | solution.py:505
  7.9 200.5 %all-gather.6.cloned.1.call-start = ((), (), s32[]{:S(2)}) async-start(), calls=%async_computation.1 | async-start | bytes 5308416 | tf_op jit(solution)/shard_map/all_gather | solution.py:506
  8.7 204.9 %all-gather.8.cloned.1.call-start = ((), (), s32[]{:S(2)}) async-start(), calls=%async_computation.2 | async-start | bytes 5308416 | tf_op jit(solution)/shard_map/all_gather | solution.py:507
  8.7 35.6 %collective-permute-start = (bf16[128,768]{1,0:T(8,128)(2,1)}, bf16[128,768]{1,0:T(8,128)(2,1)S(1)}, u32[]{:S(2)}, u32[]{:S(2)}) collective-permute-start(bf16[128,768]{1,0:T(8,128)(2,1)} %param.18), channel_id=1, source_target_pairs={{0,6},{1,7},{2,0},{3,1},{4,2},{5,3},{6,4},{7,5},{8,14},{9,15},{10,... | collective-permute-start | bytes 589832 | tf_op jit(solution)/shard_map/ppermute | solution.py:46
  12.9 31.4 %collective-permute-start.1 = (bf16[128,768]{1,0:T(8,128)(2,1)}, bf16[128,768]{1,0:T(8,128)(2,1)}, u32[]{:S(2)}, u32[]{:S(2)}) collective-permute-start(bf16[128,768]{1,0:T(8,128)(2,1)} %param.18), channel_id=1, source_target_pairs={{0,4},{1,5},{2,6},{3,7},{4,0},{5,1},{6,2},{7,3},{8,12},{9,13},{10,... | collective-permute-start | bytes 589832 | tf_op jit(solution)/shard_map/ppermute | solution.py:46
  31.9 13.4 %collective-permute-start.2 = (bf16[128,768]{1,0:T(8,128)(2,1)S(1)}, bf16[128,768]{1,0:T(8,128)(2,1)}, u32[]{:S(2)}, u32[]{:S(2)}) collective-permute-start(bf16[128,768]{1,0:T(8,128)(2,1)S(1)} %copy-done.2), channel_id=1, source_target_pairs={{0,2},{1,3},{2,4},{3,5},{4,6},{5,7},{6,0},{7,1},{8,10},{9,11},{10,... | collective-permute-start | bytes 589832 | tf_op jit(solution)/shard_map/ppermute | solution.py:46
  56.4 14.9 %collective-permute-start.9 = (bf16[512,256]{0,1:T(8,128)(2,1)S(1)}, bf16[512,256]{0,1:T(8,128)(2,1)S(1)}, u32[]{:S(2)}, u32[]{:S(2)}) collective-permute-start(bf16[512,256]{0,1:T(8,128)(2,1)S(1)} %get-tuple-element.109), channel_id=1, source_target_pairs={{0,96},{8,104},{16,112},{24,120},{32,0},{40,8},{48,16},{56,24},{64... | collective-permute-start | bytes 786440 | tf_op jit(solution)/shard_map/ppermute | solution.py:60
  59.3 12.0 %collective-permute-start.8 = (bf16[512,256]{0,1:T(8,128)(2,1)S(1)}, bf16[512,256]{0,1:T(8,128)(2,1)S(1)}, u32[]{:S(2)}, u32[]{:S(2)}) collective-permute-start(bf16[512,256]{0,1:T(8,128)(2,1)S(1)} %get-tuple-element.109), channel_id=1, source_target_pairs={{0,64},{8,72},{16,80},{24,88},{32,96},{40,104},{48,112},{56,120},{... | collective-permute-start | bytes 786440 | tf_op jit(solution)/shard_map/ppermute | solution.py:60
  60.0 14.9 %collective-permute-start.7 = (bf16[512,256]{0,1:T(8,128)(2,1)S(1)}, bf16[512,256]{0,1:T(8,128)(2,1)S(1)}, u32[]{:S(2)}, u32[]{:S(2)}) collective-permute-start(bf16[512,256]{0,1:T(8,128)(2,1)S(1)} %get-tuple-element.109), channel_id=1, source_target_pairs={{0,32},{8,40},{16,48},{24,56},{32,64},{40,72},{48,80},{56,88},{64,... | collective-permute-start | bytes 786440 | tf_op jit(solution)/shard_map/ppermute | solution.py:60
  76.9 30.6 %collective-permute-start.10 = (bf16[4,512,256]{1,2,0:T(8,128)(2,1)S(1)}, bf16[4,512,256]{1,2,0:T(8,128)(2,1)}, u32[]{:S(2)}, u32[]{:S(2)}) collective-permute-start(bf16[4,512,256]{1,2,0:T(8,128)(2,1)S(1)} %pad_maximum_fusion.2), channel_id=1, source_target_pairs={{0,1},{1,0},{2,3},{3,2},{4,5},{5,4},{6,7},{7,6},{8,9},{9,8},{10,11... | collective-permute-start | bytes 3145736 | tf_op jit(solution)/shard_map/ppermute | solution.py:50
  78.0 20.8 %collective-permute-start.13 = (bf16[512,384]{0,1:T(8,128)(2,1)}, bf16[512,384]{0,1:T(8,128)(2,1)S(1)}, u32[]{:S(2)}, u32[]{:S(2)}) collective-permute-start(bf16[512,384]{0,1:T(8,128)(2,1)} %pad_maximum_fusion.7), channel_id=1, source_target_pairs={{0,24},{8,0},{16,8},{24,16},{32,56},{40,32},{48,40},{56,48},{64,88... | collective-permute-start | bytes 1179656 | tf_op jit(solution)/shard_map/ppermute | solution.py:55
  81.0 17.8 %collective-permute-start.12 = (bf16[512,384]{0,1:T(8,128)(2,1)}, bf16[512,384]{0,1:T(8,128)(2,1)}, u32[]{:S(2)}, u32[]{:S(2)}) collective-permute-start(bf16[512,384]{0,1:T(8,128)(2,1)} %pad_maximum_fusion.7), channel_id=1, source_target_pairs={{0,16},{8,24},{16,0},{24,8},{32,48},{40,56},{48,32},{56,40},{64,80... | collective-permute-start | bytes 1179656 | tf_op jit(solution)/shard_map/ppermute | solution.py:55
  81.8 20.7 %collective-permute-start.11 = (bf16[512,384]{0,1:T(8,128)(2,1)}, bf16[512,384]{0,1:T(8,128)(2,1)}, u32[]{:S(2)}, u32[]{:S(2)}) collective-permute-start(bf16[512,384]{0,1:T(8,128)(2,1)} %pad_maximum_fusion.7), channel_id=1, source_target_pairs={{0,8},{8,16},{16,24},{24,0},{32,40},{40,48},{48,56},{56,32},{64,72... | collective-permute-start | bytes 1179656 | tf_op jit(solution)/shard_map/ppermute | solution.py:55
  155.3 12.0 %collective-permute-start.14 = (bf16[8,256,256]{2,1,0:T(8,128)(2,1)S(1)}, bf16[8,256,256]{2,1,0:T(8,128)(2,1)S(1)}, u32[]{:S(2)}, u32[]{:S(2)}) collective-permute-start(bf16[8,256,256]{2,1,0:T(8,128)(2,1)S(1)} %get-tuple-element.23), channel_id=1, source_target_pairs={{0,1},{1,0},{2,3},{3,2},{4,5},{5,4},{6,7},{7,6},{8,9},{9,8},{10,11... | collective-permute-start | bytes 3145736 | tf_op jit(solution)/shard_map/ppermute | solution.py:50
  158.9 14.3 %collective-permute-start.59 = (bf16[128,768]{1,0:T(8,128)(2,1)S(1)}, bf16[128,768]{1,0:T(8,128)(2,1)}, u32[]{:S(2)}, u32[]{:S(2)}) collective-permute-start(bf16[128,768]{1,0:T(8,128)(2,1)S(1)} %copy-done.15), channel_id=1, source_target_pairs={{0,2},{1,3},{2,4},{3,5},{4,6},{5,7},{6,0},{7,1},{8,10},{9,11},{10,... | collective-permute-start | bytes 589832 | tf_op jit(solution)/shard_map/ppermute | solution.py:46
  171.6 10.7 %collective-permute-start.16 = (bf16[512,256]{1,0:T(8,128)(2,1)S(1)}, bf16[512,256]{1,0:T(8,128)(2,1)S(1)}, u32[]{:S(2)}, u32[]{:S(2)}) collective-permute-start(bf16[512,256]{1,0:T(8,128)(2,1)S(1)} %get-tuple-element.70), channel_id=1, source_target_pairs={{0,64},{8,72},{16,80},{24,88},{32,96},{40,104},{48,112},{56,120},{... | collective-permute-start | bytes 786440 | tf_op jit(solution)/shard_map/ppermute | solution.py:60
  172.4 12.8 %collective-permute-start.17 = (bf16[512,256]{1,0:T(8,128)(2,1)S(1)}, bf16[512,256]{1,0:T(8,128)(2,1)S(1)}, u32[]{:S(2)}, u32[]{:S(2)}) collective-permute-start(bf16[512,256]{1,0:T(8,128)(2,1)S(1)} %get-tuple-element.69), channel_id=1, source_target_pairs={{0,32},{8,40},{16,48},{24,56},{32,64},{40,72},{48,80},{56,88},{64,... | collective-permute-start | bytes 786440 | tf_op jit(solution)/shard_map/ppermute | solution.py:60
  222.4 69.4 %collective-permute-start.60 = (bf16[128,768]{1,0:T(8,128)(2,1)S(1)}, bf16[128,768]{1,0:T(8,128)(2,1)}, u32[]{:S(2)}, u32[]{:S(2)}) collective-permute-start(bf16[128,768]{1,0:T(8,128)(2,1)S(1)} %get-tuple-element.40), channel_id=1, source_target_pairs={{0,6},{1,7},{2,0},{3,1},{4,2},{5,3},{6,4},{7,5},{8,14},{9,15},{10,... | collective-permute-start | bytes 589832 | tf_op jit(solution)/shard_map/ppermute | solution.py:46
  224.1 68.7 %collective-permute-start.61 = (bf16[128,768]{1,0:T(8,128)(2,1)S(1)}, bf16[128,768]{1,0:T(8,128)(2,1)}, u32[]{:S(2)}, u32[]{:S(2)}) collective-permute-start(bf16[128,768]{1,0:T(8,128)(2,1)S(1)} %get-tuple-element.40), channel_id=1, source_target_pairs={{0,4},{1,5},{2,6},{3,7},{4,0},{5,1},{6,2},{7,3},{8,12},{9,13},{10,... | collective-permute-start | bytes 589832 | tf_op jit(solution)/shard_map/ppermute | solution.py:46
  224.6 70.0 %collective-permute-start.62 = (bf16[128,768]{1,0:T(8,128)(2,1)S(1)}, bf16[128,768]{1,0:T(8,128)(2,1)}, u32[]{:S(2)}, u32[]{:S(2)}) collective-permute-start(bf16[128,768]{1,0:T(8,128)(2,1)S(1)} %get-tuple-element.40), channel_id=1, source_target_pairs={{0,2},{1,3},{2,4},{3,5},{4,6},{5,7},{6,0},{7,1},{8,10},{9,11},{10,... | collective-permute-start | bytes 589832 | tf_op jit(solution)/shard_map/ppermute | solution.py:46
  225.0 79.9 %collective-permute-start.66 = (bf16[128,3072]{1,0:T(8,128)(2,1)S(1)}, bf16[128,3072]{1,0:T(8,128)(2,1)}, u32[]{:S(2)}, u32[]{:S(2)}) collective-permute-start(bf16[128,3072]{1,0:T(8,128)(2,1)S(1)} %get-tuple-element.38), channel_id=1, source_target_pairs={{0,6},{1,7},{2,0},{3,1},{4,2},{5,3},{6,4},{7,5},{8,14},{9,15},{10,... | collective-permute-start | bytes 2359304 | tf_op jit(solution)/shard_map/ppermute | solution.py:46
  229.3 19.2 %collective-permute-start.21 = (bf16[128,192]{0,1:T(8,128)(2,1)S(1)}, bf16[128,192]{0,1:T(8,128)(2,1)S(1)}, u32[]{:S(2)}, u32[]{:S(2)}) collective-permute-start(bf16[128,192]{0,1:T(8,128)(2,1)S(1)} %get-tuple-element.107), channel_id=1, source_target_pairs={{0,6},{1,7},{2,0},{3,1},{4,2},{5,3},{6,4},{7,5},{8,14},{9,15},{10,... | collective-permute-start | bytes 147464 | tf_op jit(solution)/shard_map/ppermute | solution.py:46
  275.8 14.5 %collective-permute-start.56 = (bf16[128,768]{0,1:T(8,128)(2,1)S(1)}, bf16[128,768]{0,1:T(8,128)(2,1)S(1)}, u32[]{:S(2)}, u32[]{:S(2)}) collective-permute-start(bf16[128,768]{0,1:T(8,128)(2,1)S(1)} %bitcast.403), channel_id=1, source_target_pairs={{0,2},{1,3},{2,4},{3,5},{4,6},{5,7},{6,0},{7,1},{8,10},{9,11},{10,... | collective-permute-start | bytes 589832 | tf_op jit(solution)/shard_map/ppermute | solution.py:46
  290.3 18.1 %collective-permute-start.67 = (bf16[128,3072]{1,0:T(8,128)(2,1)S(1)}, bf16[128,3072]{1,0:T(8,128)(2,1)S(1)}, u32[]{:S(2)}, u32[]{:S(2)}) collective-permute-start(bf16[128,3072]{1,0:T(8,128)(2,1)S(1)} %get-tuple-element.38), channel_id=1, source_target_pairs={{0,4},{1,5},{2,6},{3,7},{4,0},{5,1},{6,2},{7,3},{8,12},{9,13},{10,... | collective-permute-start | bytes 2359304 | tf_op jit(solution)/shard_map/ppermute | solution.py:46
  291.8 11.5 %collective-permute-start.26 = (bf16[512,256]{1,0:T(8,128)(2,1)S(1)}, bf16[512,256]{1,0:T(8,128)(2,1)S(1)}, u32[]{:S(2)}, u32[]{:S(2)}) collective-permute-start(bf16[512,256]{1,0:T(8,128)(2,1)S(1)} %pack_context_gradient.1), channel_id=1, source_target_pairs={{0,96},{8,104},{16,112},{24,120},{32,0},{40,8},{48,16},{56,24},{64... | collective-permute-start | bytes 786440 | tf_op jit(solution)/shard_map/ppermute | solution.py:60
  292.8 10.8 %collective-permute-start.25 = (bf16[512,256]{1,0:T(8,128)(2,1)S(1)}, bf16[512,256]{1,0:T(8,128)(2,1)S(1)}, u32[]{:S(2)}, u32[]{:S(2)}) collective-permute-start(bf16[512,256]{1,0:T(8,128)(2,1)S(1)} %pack_context_gradient.1), channel_id=1, source_target_pairs={{0,64},{8,72},{16,80},{24,88},{32,96},{40,104},{48,112},{56,120},{... | collective-permute-start | bytes 786440 | tf_op jit(solution)/shard_map/ppermute | solution.py:60
  303.2 13.6 %collective-permute-start.68 = (bf16[128,3072]{1,0:T(8,128)(2,1)S(1)}, bf16[128,3072]{1,0:T(8,128)(2,1)S(1)}, u32[]{:S(2)}, u32[]{:S(2)}) collective-permute-start(bf16[128,3072]{1,0:T(8,128)(2,1)S(1)} %get-tuple-element.38), channel_id=1, source_target_pairs={{0,2},{1,3},{2,4},{3,5},{4,6},{5,7},{6,0},{7,1},{8,10},{9,11},{10,... | collective-permute-start | bytes 2359304 | tf_op jit(solution)/shard_map/ppermute | solution.py:46
  304.8 22.3 %collective-permute-start.27 = (bf16[4,512,256]{2,1,0:T(8,128)(2,1)}, bf16[4,512,256]{2,1,0:T(8,128)(2,1)}, u32[]{:S(2)}, u32[]{:S(2)}) collective-permute-start(bf16[4,512,256]{2,1,0:T(8,128)(2,1)} %pad_maximum_fusion.3), channel_id=1, source_target_pairs={{0,1},{1,0},{2,3},{3,2},{4,5},{5,4},{6,7},{7,6},{8,9},{9,8},{10,11... | collective-permute-start | bytes 3145736 | tf_op jit(solution)/shard_map/ppermute | solution.py:50
  323.3 73.5 %collective-permute-start.69 = (bf16[864,768]{1,0:T(8,128)(2,1)}, bf16[864,768]{1,0:T(8,128)(2,1)}, u32[]{:S(2)}, u32[]{:S(2)}) collective-permute-start(bf16[864,768]{1,0:T(8,128)(2,1)} %constant_dynamic-update-slice_fusion.65), channel_id=1, source_target_pairs={{0,1},{1,0},{2,3},{3,2},{4,5},{5,4},{6,7},{7,6},{8,9},{9,8},{10,11... | collective-permute-start | bytes 3981320 | tf_op jit(solution)/shard_map/ppermute | solution.py:50
  393.3 20.9 %collective-permute-start.34 = (bf16[512,384]{1,0:T(8,128)(2,1)S(1)}, bf16[512,384]{1,0:T(8,128)(2,1)S(1)}, u32[]{:S(2)}, u32[]{:S(2)}) collective-permute-start(bf16[512,384]{1,0:T(8,128)(2,1)S(1)} %bitcast.392), channel_id=1, source_target_pairs={{0,8},{8,16},{16,24},{24,0},{32,40},{40,48},{48,56},{56,32},{64,72... | collective-permute-start | bytes 1179656 | tf_op jit(solution)/shard_map/ppermute | solution.py:55
  393.3 21.0 %collective-permute-start.33 = (bf16[512,384]{1,0:T(8,128)(2,1)S(1)}, bf16[512,384]{1,0:T(8,128)(2,1)S(1)}, u32[]{:S(2)}, u32[]{:S(2)}) collective-permute-start(bf16[512,384]{1,0:T(8,128)(2,1)S(1)} %bitcast.391), channel_id=1, source_target_pairs={{0,16},{8,24},{16,0},{24,8},{32,48},{40,56},{48,32},{56,40},{64,80... | collective-permute-start | bytes 1179656 | tf_op jit(solution)/shard_map/ppermute | solution.py:55
  395.3 22.6 %collective-permute-start.32 = (bf16[512,384]{1,0:T(8,128)(2,1)}, bf16[512,384]{1,0:T(8,128)(2,1)}, u32[]{:S(2)}, u32[]{:S(2)}) collective-permute-start(bf16[512,384]{1,0:T(8,128)(2,1)} %bitcast.56), channel_id=1, source_target_pairs={{0,24},{8,0},{16,8},{24,16},{32,56},{40,32},{48,40},{56,48},{64,88... | collective-permute-start | bytes 1179656 | tf_op jit(solution)/shard_map/ppermute | solution.py:55
  396.8 42.8 %collective-permute-start.28 = (bf16[8,256,256]{2,1,0:T(8,128)(2,1)}, bf16[8,256,256]{2,1,0:T(8,128)(2,1)}, u32[]{:S(2)}, u32[]{:S(2)}) collective-permute-start(bf16[8,256,256]{2,1,0:T(8,128)(2,1)} %get-tuple-element.25), channel_id=1, source_target_pairs={{0,1},{1,0},{2,3},{3,2},{4,5},{5,4},{6,7},{7,6},{8,9},{9,8},{10,11... | collective-permute-start | bytes 3145736 | tf_op jit(solution)/shard_map/ppermute | solution.py:50
  399.6 23.7 %collective-permute-start.72 = (bf16[224,768]{1,0:T(8,128)(2,1)}, bf16[224,768]{1,0:T(8,128)(2,1)}, u32[]{:S(2)}, u32[]{:S(2)}) collective-permute-start(bf16[224,768]{1,0:T(8,128)(2,1)} %get-tuple-element.58), channel_id=1, source_target_pairs={{0,24},{8,0},{16,8},{24,16},{32,56},{40,32},{48,40},{56,48},{64,88... | collective-permute-start | bytes 1032200 | tf_op jit(solution)/shard_map/ppermute | solution.py:55
  414.2 12.9 %collective-permute-start.71 = (bf16[224,768]{1,0:T(8,128)(2,1)}, bf16[224,768]{1,0:T(8,128)(2,1)}, u32[]{:S(2)}, u32[]{:S(2)}) collective-permute-start(bf16[224,768]{1,0:T(8,128)(2,1)} %get-tuple-element.59), channel_id=1, source_target_pairs={{0,16},{8,24},{16,0},{24,8},{32,48},{40,56},{48,32},{56,40},{64,80... | collective-permute-start | bytes 1032200 | tf_op jit(solution)/shard_map/ppermute | solution.py:55
  415.7 17.2 %collective-permute-start.70 = (bf16[224,768]{1,0:T(8,128)(2,1)}, bf16[224,768]{1,0:T(8,128)(2,1)}, u32[]{:S(2)}, u32[]{:S(2)}) collective-permute-start(bf16[224,768]{1,0:T(8,128)(2,1)} %get-tuple-element.57), channel_id=1, source_target_pairs={{0,8},{8,16},{16,24},{24,0},{32,40},{40,48},{48,56},{56,32},{64,72... | collective-permute-start | bytes 1032200 | tf_op jit(solution)/shard_map/ppermute | solution.py:55
  444.9 19.4 %collective-permute-start.31 = (bf16[512,256]{1,0:T(8,128)(2,1)S(1)}, bf16[512,256]{1,0:T(8,128)(2,1)S(1)}, u32[]{:S(2)}, u32[]{:S(2)}) collective-permute-start(bf16[512,256]{1,0:T(8,128)(2,1)S(1)} %bitcast.400), channel_id=1, source_target_pairs={{0,32},{8,40},{16,48},{24,56},{32,64},{40,72},{48,80},{56,88},{64,... | collective-permute-start | bytes 786440 | tf_op jit(solution)/shard_map/ppermute | solution.py:60
  446.7 17.6 %collective-permute-start.30 = (bf16[512,256]{1,0:T(8,128)(2,1)S(1)}, bf16[512,256]{1,0:T(8,128)(2,1)S(1)}, u32[]{:S(2)}, u32[]{:S(2)}) collective-permute-start(bf16[512,256]{1,0:T(8,128)(2,1)S(1)} %bitcast.398), channel_id=1, source_target_pairs={{0,64},{8,72},{16,80},{24,88},{32,96},{40,104},{48,112},{56,120},{... | collective-permute-start | bytes 786440 | tf_op jit(solution)/shard_map/ppermute | solution.py:60
  448.0 16.4 %collective-permute-start.29 = (bf16[512,256]{1,0:T(8,128)(2,1)S(1)}, bf16[512,256]{1,0:T(8,128)(2,1)S(1)}, u32[]{:S(2)}, u32[]{:S(2)}) collective-permute-start(bf16[512,256]{1,0:T(8,128)(2,1)S(1)} %bitcast.396), channel_id=1, source_target_pairs={{0,96},{8,104},{16,112},{24,120},{32,0},{40,8},{48,16},{56,24},{64... | collective-permute-start | bytes 786440 | tf_op jit(solution)/shard_map/ppermute | solution.py:60
  449.5 12.3 %collective-permute-start.77 = (bf16[56,768]{1,0:T(8,128)(2,1)S(1)}, bf16[56,768]{1,0:T(8,128)(2,1)S(1)}, u32[]{:S(2)}, u32[]{:S(2)}) collective-permute-start(bf16[56,768]{1,0:T(8,128)(2,1)S(1)} %get-tuple-element.36), channel_id=1, source_target_pairs={{0,64},{8,72},{16,80},{24,88},{32,96},{40,104},{48,112},{56,120},{... | collective-permute-start | bytes 258056 | tf_op jit(solution)/shard_map/ppermute | solution.py:60
  451.2 11.8 %collective-permute-start.78 = (bf16[56,768]{1,0:T(8,128)(2,1)S(1)}, bf16[56,768]{1,0:T(8,128)(2,1)S(1)}, u32[]{:S(2)}, u32[]{:S(2)}) collective-permute-start(bf16[56,768]{1,0:T(8,128)(2,1)S(1)} %get-tuple-element.36), channel_id=1, source_target_pairs={{0,32},{8,40},{16,48},{24,56},{32,64},{40,72},{48,80},{56,88},{64,... | collective-permute-start | bytes 258056 | tf_op jit(solution)/shard_map/ppermute | solution.py:60
  463.1 21.5 %collective-permute-start.79 = (bf16[224,768]{1,0:T(8,128)(2,1)S(1)}, bf16[224,768]{1,0:T(8,128)(2,1)S(1)}, u32[]{:S(2)}, u32[]{:S(2)}) collective-permute-start(bf16[224,768]{1,0:T(8,128)(2,1)S(1)} %bitcast.359), channel_id=1, source_target_pairs={{0,24},{8,0},{16,8},{24,16},{32,56},{40,32},{48,40},{56,48},{64,88... | collective-permute-start | bytes 1032200 | tf_op jit(solution)/shard_map/ppermute | solution.py:55
  463.2 23.1 %collective-permute-start.80 = (bf16[224,768]{1,0:T(8,128)(2,1)S(1)}, bf16[224,768]{1,0:T(8,128)(2,1)S(1)}, u32[]{:S(2)}, u32[]{:S(2)}) collective-permute-start(bf16[224,768]{1,0:T(8,128)(2,1)S(1)} %bitcast.360), channel_id=1, source_target_pairs={{0,16},{8,24},{16,0},{24,8},{32,48},{40,56},{48,32},{56,40},{64,80... | collective-permute-start | bytes 1032200 | tf_op jit(solution)/shard_map/ppermute | solution.py:55
  474.3 27.7 %collective-permute-start.81 = (bf16[224,768]{1,0:T(8,128)(2,1)S(1)}, bf16[224,768]{1,0:T(8,128)(2,1)}, u32[]{:S(2)}, u32[]{:S(2)}) collective-permute-start(bf16[224,768]{1,0:T(8,128)(2,1)S(1)} %bitcast.362), channel_id=1, source_target_pairs={{0,8},{8,16},{16,24},{24,0},{32,40},{40,48},{48,56},{56,32},{64,72... | collective-permute-start | bytes 1032200 | tf_op jit(solution)/shard_map/ppermute | solution.py:55
  482.9 10.4 %collective-permute-start.39 = (bf16[196,576]{1,0:T(8,128)(2,1)S(1)}, bf16[196,576]{1,0:T(8,128)(2,1)S(1)}, u32[]{:S(2)}, u32[]{:S(2)}) collective-permute-start(bf16[196,576]{1,0:T(8,128)(2,1)S(1)} %get-tuple-element.74), channel_id=1, source_target_pairs={{0,4},{1,5},{2,6},{3,7},{4,0},{5,1},{6,2},{7,3},{8,12},{9,13},{10,... | collective-permute-start | bytes 677384 | tf_op jit(solution)/shard_map/ppermute | solution.py:46
  484.6 11.3 %collective-permute-start.40 = (bf16[196,576]{1,0:T(8,128)(2,1)S(1)}, bf16[196,576]{1,0:T(8,128)(2,1)S(1)}, u32[]{:S(2)}, u32[]{:S(2)}) collective-permute-start(bf16[196,576]{1,0:T(8,128)(2,1)S(1)} %get-tuple-element.75), channel_id=1, source_target_pairs={{0,2},{1,3},{2,4},{3,5},{4,6},{5,7},{6,0},{7,1},{8,10},{9,11},{10,... | collective-permute-start | bytes 677384 | tf_op jit(solution)/shard_map/ppermute | solution.py:46
  505.5 11.4 %collective-permute-start.44 = (bf16[128,576]{1,0:T(8,128)(2,1)S(1)}, bf16[128,576]{1,0:T(8,128)(2,1)S(1)}, u32[]{:S(2)}, u32[]{:S(2)}) collective-permute-start(bf16[128,576]{1,0:T(8,128)(2,1)S(1)} %get-tuple-element.88), channel_id=1, source_target_pairs={{0,24},{8,0},{16,8},{24,16},{32,56},{40,32},{48,40},{56,48},{64,88... | collective-permute-start | bytes 442376 | tf_op jit(solution)/shard_map/ppermute | solution.py:55
  509.3 11.0 %collective-permute-start.42 = (bf16[128,576]{1,0:T(8,128)(2,1)S(1)}, bf16[128,576]{1,0:T(8,128)(2,1)S(1)}, u32[]{:S(2)}, u32[]{:S(2)}) collective-permute-start(bf16[128,576]{1,0:T(8,128)(2,1)S(1)} %get-tuple-element.87), channel_id=1, source_target_pairs={{0,8},{8,16},{16,24},{24,0},{32,40},{40,48},{48,56},{56,32},{64,72... | collective-permute-start | bytes 442376 | tf_op jit(solution)/shard_map/ppermute | solution.py:55
  (88 other events, 646.3 us)
Sparse Core Ops, SparseCore 0:
  9.7 27.8 all-gather.3
  39.3 34.5 all-gather.5
  75.6 34.5 all-gather.7
